TPU v7x, 128 devices: a whole 4x4x4 slice. The times are simulated.
128 devices in a mesh: grp: 16 (over z, x), in: 8 (over y, core).
Axes of the slice: x: 4, y: 4, z: 4, core: 2. Of those that a mesh axis runs over, the one named last changes fastest.
Arguments:
- encoded: bfloat16 [16384, 1024], P(('grp', 'in')), may hold values from -6 to 6
- owner_slot: int32 [16384], P(('grp', 'in')), may hold values from 0 to 16383, as said below
- label_mask: int32 [16384], P(('grp', 'in')), may hold values 0 or 1
- cotangent: bfloat16 [16384, 1024], P(('grp', 'in')), may hold values from -6 to 6
- weight: bfloat16 [1024, 1024], P(('grp', 'in')), may hold values from -0.1875 to 0.1875
- block_cols: int32 [128, 10], P(('grp', 'in')), may hold values from 0 to 7, as said below
- block_counts: int32 [128], P(('grp', 'in')), may hold values from 1 to 10, as said below
- block_values: bfloat16 [128, 10, 128, 128], P(('grp', 'in')), as said below
Outputs:
- layer_out: bfloat16 [16384, 1024], P(('grp', 'in'))
- encoded_grad: bfloat16 [16384, 1024], P(('grp', 'in'))
- weight_grad: float32 [1024, 1024], P(('grp', 'in'))
Inputs may be any that keep to these rules, and one draw needn't show every extreme that they name: A permutation of the nodes. The owner of node i is owner_slot[i] // 128; from the nodes of one device at most 2 go to one owner, and every device sends exactly 2 to some owner. `block_cols`: slot 0 of every block-row names the block-row itself; slots at or past block_counts are unused. adjacency is symmetric. `block_counts`: every partition group has a block-row with 10 slots in use. `block_values`: the blocks make adjacency symmetric.
All inputs are finite; a program needn't handle non-finite values. No bound on the sum of `label_mask` on one device may be relied on, other than what follows from the above.
Results may differ from a plain program's by a relative error of at most 0.0063.
Values may be sent and summed in bfloat16 or wider, within the bound.
A program may use at most 64 MiB of HBM per device.

v0:
```python
import jax
import jax.numpy as jnp
from jax import lax
from jax.sharding import PartitionSpec as P


def smooth_gate(values):
    return jax.nn.gelu(values, approximate=True)


def to_owners(send_rows, send_cot, send_place):
    return (
        lax.all_to_all(send_rows, ("grp", "in"), split_axis=0, concat_axis=0, tiled=True),
        lax.all_to_all(send_cot, ("grp", "in"), split_axis=0, concat_axis=0, tiled=True),
        lax.all_to_all(send_place, ("grp", "in"), split_axis=0, concat_axis=0, tiled=True),
    )


def to_sources(out_back, grad_back):
    return (
        lax.all_to_all(out_back, ("grp", "in"), split_axis=0, concat_axis=0, tiled=True),
        lax.all_to_all(grad_back, ("grp", "in"), split_axis=0, concat_axis=0, tiled=True),
    )


def propagate(own_rows, block_cols, masked):
    block_rows, slot_count, block_size, _ = masked.shape
    feat_width = own_rows.shape[1]
    gathered = lax.all_gather(own_rows, "in", axis=0, tiled=True)
    pieces = gathered.reshape(-1, block_size, feat_width)[block_cols]
    mixed_block = jnp.einsum("bkpq,bkqd->bpd", masked, pieces, preferred_element_type=jnp.float32)
    return mixed_block.reshape(-1, feat_width)


def per_device(
    encoded, owner_slot, label_mask, cotangent, weight, block_cols, block_counts, block_values
):
    grp_size = lax.axis_size("grp")
    in_size = lax.axis_size("in")
    owners = grp_size * in_size
    row_count, feat_width = encoded.shape
    slot_room = 2 * row_count // owners
    target_rows = owner_slot // row_count
    local_place = owner_slot % row_count
    member = (target_rows[:, None] == jnp.arange(owners, dtype=jnp.int32)[None, :]).astype(
        jnp.int32
    )
    row_rank = jnp.sum(jnp.cumsum(member, axis=0) * member, axis=1) - 1
    slot_flat = target_rows * slot_room + row_rank
    labelled = jnp.where(label_mask[:, None] > 0, cotangent, jnp.zeros_like(cotangent))
    send_rows = jnp.zeros((owners * slot_room, feat_width), jnp.bfloat16).at[slot_flat].set(encoded)
    send_cot = jnp.zeros((owners * slot_room, feat_width), jnp.bfloat16).at[slot_flat].set(labelled)
    send_place = (
        jnp.full((owners * slot_room,), row_count, jnp.int32).at[slot_flat].set(local_place)
    )
    recv_rows, recv_cot, recv_place = to_owners(
        send_rows.reshape(owners, slot_room, feat_width),
        send_cot.reshape(owners, slot_room, feat_width),
        send_place.reshape(owners, slot_room),
    )
    recv_rows = recv_rows.reshape(-1, feat_width)
    recv_cot = recv_cot.reshape(-1, feat_width)
    recv_place = recv_place.reshape(-1)
    own_rows = (
        jnp.zeros((row_count, feat_width), jnp.bfloat16).at[recv_place].set(recv_rows, mode="drop")
    )
    own_cot = (
        jnp.zeros((row_count, feat_width), jnp.bfloat16).at[recv_place].set(recv_cot, mode="drop")
    )
    whole_weight = lax.all_gather(weight, ("grp", "in"), axis=0, tiled=True)
    slot_count = block_values.shape[1]
    live_slot = jnp.arange(slot_count, dtype=jnp.int32)[None, :] < block_counts[:, None]
    masked = jnp.where(live_slot[:, :, None, None], block_values, jnp.zeros_like(block_values))
    mixed_rows = propagate(own_rows, block_cols, masked).astype(jnp.bfloat16)
    pre_act = jnp.dot(mixed_rows, whole_weight, preferred_element_type=jnp.float32)
    activated, pullback = jax.vjp(smooth_gate, pre_act)
    out_own = activated.astype(jnp.bfloat16)
    grad_pre = pullback(own_cot.astype(jnp.float32))[0].astype(jnp.bfloat16)
    weight_grad = (
        lax.psum_scatter(
            lax.dot_general(
                mixed_rows, grad_pre, (((0,), (0,)), ((), ())), preferred_element_type=jnp.float32
            ),
            ("grp", "in"),
            scatter_dimension=0,
            tiled=True,
        )
        / owners
    )
    grad_feed = lax.dot_general(
        grad_pre, whole_weight, (((1,), (1,)), ((), ())), preferred_element_type=jnp.float32
    ).astype(jnp.bfloat16)
    grad_own = propagate(grad_feed, block_cols, masked).astype(jnp.bfloat16)
    filled = recv_place < row_count
    clipped = jnp.minimum(recv_place, row_count - 1)
    out_back = jnp.where(filled[:, None], out_own[clipped], jnp.zeros((), jnp.bfloat16))
    grad_back = jnp.where(filled[:, None], grad_own[clipped], jnp.zeros((), jnp.bfloat16))
    ret_out, ret_grad = to_sources(
        out_back.reshape(owners, slot_room, feat_width),
        grad_back.reshape(owners, slot_room, feat_width),
    )
    layer_out = ret_out.reshape(-1, feat_width)[slot_flat]
    encoded_grad = ret_grad.reshape(-1, feat_width)[slot_flat]
    return (layer_out, encoded_grad, weight_grad)


def solution(mesh):
    in_specs = (
        P(("grp", "in"), None),
        P(("grp", "in")),
        P(("grp", "in")),
        P(("grp", "in"), None),
        P(("grp", "in"), None),
        P(("grp", "in"), None),
        P(("grp", "in")),
        P(("grp", "in"), None, None, None),
    )
    out_specs = (P(("grp", "in"), None), P(("grp", "in"), None), P(("grp", "in"), None))
    return jax.shard_map(
        per_device, mesh=mesh, in_specs=in_specs, out_specs=out_specs, check_vma=False
    )
```

profile of v0, /device:TPU:1, one launch (start us, length us, event | category | flops | bytes accessed | tf_op | source)
XLA Modules:
  0.0 821.0 jit_solution(15428504078395396005)
XLA Ops:
  10.1 11.5 %all-to-all-start = ((s32[128,1,2]{2,1,0:T(1,128)}), s32[128,1,2]{2,1,0:T(1,128)S(1)}, u32[]{:S(2)}, u32[]{:S(2)}) async-start(s32[128,1,2]{2,1,0:T(1,128)} %bitcast), calls=%async_computation | async-start | bytes 131072 | tf_op jit(solution)/shard_map/all_to_all | solution.py:15
  21.6 1.7 scatter_custom_fusion.1
  24.3 6.8 all-to-all-done
  31.1 4.4 all-to-all-start.1
  37.1 12.0 %all-to-all-done.1 = bf16[128,2,1024]{2,1,0:T(2,128)(2,1)S(1)} async-done(((bf16[128,2,1024]{2,1,0:T(2,128)(2,1)}), bf16[128,2,1024]{2,1,0:T(2,128)(2,1)S(1)}, u32[]{:S(2)}, u32[]{:S(2)}) %all-to-all-start.1) | async-done | bytes 524320 | tf_op jit(solution)/shard_map/all_to_all | solution.py:13
  49.3 2.3 scatter_custom_fusion.2
  54.8 4.6 all-to-all-start.3
  60.1 12.9 %all-to-all-done.3 = bf16[128,2,1024]{2,1,0:T(2,128)(2,1)S(1)} async-done(((bf16[128,2,1024]{2,1,0:T(2,128)(2,1)}), bf16[128,2,1024]{2,1,0:T(2,128)(2,1)S(1)}, u32[]{:S(2)}, u32[]{:S(2)}) %all-to-all-start.3) | async-done | bytes 524320 | tf_op jit(solution)/shard_map/all_to_all | solution.py:14
  73.2 2.3 scatter_custom_fusion.4
  75.5 3.0 all-gather.4.cloned.1.call-done
  78.5 2.4 gather_fusion
  81.4 66.5 %all-gather.6.cloned.1.call-done = bf16[1024,1024]{1,0:T(8,128)(2,1)} async-done(((bf16[8,1024]{1,0:T(8,128)(2,1)}), bf16[1024,1024]{1,0:T(8,128)(2,1)}) %all-gather.6.cloned.1.call-update) | async-done | bytes 2097168 | tf_op jit(solution)/shard_map/all_gather | solution.py:70
  148.0 2.2 multiply_convert_fusion
  150.3 1.6 convolution_convert_fusion
  152.2 2.8 fusion.31
  156.6 18.1 %all-gather.8.cloned.1.call-done = bf16[1024,1024]{1,0:T(8,128)(2,1)} async-done(((bf16[128,1024]{1,0:T(8,128)(2,1)}), bf16[1024,1024]{1,0:T(8,128)(2,1)}) %all-gather.8.cloned.1.call-update) | async-done | bytes 2097168 | tf_op jit(solution)/shard_map/all_gather | solution.py:29
  174.7 2.3 gather_fusion.3
  179.9 1.8 broadcast_select_fusion
  181.8 21.5 %all_to_all.29 = bf16[128,2,1024]{2,1,0:T(2,128)(2,1)S(1)} all-to-all(bf16[128,2,1024]{2,1,0:T(2,128)(2,1)S(1)} %get-tuple-element.3), channel_id=1, replica_groups=mesh['grp'=16,'in'=8] {'grp','in'}, dimensions={0} | all-to-all | bytes 1048576 | tf_op jit(solution)/shard_map/all_to_all | solution.py:22
  203.3 4.7 all-to-all-start.2
  208.3 1.6 gather_fusion.5
  209.8 12.1 %all-to-all-done.2 = bf16[128,2,1024]{2,1,0:T(2,128)(2,1)S(1)} async-done(((bf16[128,2,1024]{2,1,0:T(2,128)(2,1)}), bf16[128,2,1024]{2,1,0:T(2,128)(2,1)S(1)}, u32[]{:S(2)}, u32[]{:S(2)}) %all-to-all-start.2) | async-done | bytes 524320 | tf_op jit(solution)/shard_map/all_to_all | solution.py:21
  222.1 1.6 gather_fusion.2
  223.7 589.5 %reduce-scatter.2.cloned.1.call-done = f32[8,1024]{1,0:T(8,128)} async-done(((f32[1024,1024]{1,0:T(8,128)}), f32[8,1024]{1,0:T(8,128)}) %reduce-scatter.2.cloned.1.call-update) | async-done | bytes 32784 | tf_op jit(solution)/shard_map/reduce_scatter | solution.py:80
  (54 shorter events, 16.1 us)
Async XLA Ops:
  7.2 45.2 %copy-start.4 = (s32[128]{0:T(128)S(1)}, s32[128]{0:T(128)}, u32[]{:S(2)}) copy-start(s32[128]{0:T(128)} %param.10) | copy-start | bytes 1540
  7.2 45.2 %copy-start.2 = (bf16[128,1024]{1,0:T(8,128)(2,1)S(1)}, bf16[128,1024]{1,0:T(8,128)(2,1)}, u32[]{:S(2)}) copy-start(bf16[128,1024]{1,0:T(8,128)(2,1)} %param.11) | copy-start | bytes 786436
  10.1 21.0 %all-to-all-start = ((s32[128,1,2]{2,1,0:T(1,128)}), s32[128,1,2]{2,1,0:T(1,128)S(1)}, u32[]{:S(2)}, u32[]{:S(2)}) async-start(s32[128,1,2]{2,1,0:T(1,128)} %bitcast), calls=%async_computation | async-start | bytes 131072 | tf_op jit(solution)/shard_map/all_to_all | solution.py:15
  24.3 35.7 %copy-start.5 = (s32[1,10]{1,0:T(1,128)S(1)}, s32[1,10]{1,0:T(1,128)}, u32[]{:S(2)}) copy-start(s32[1,10]{1,0:T(1,128)} %param.13) | copy-start | bytes 124
  31.1 17.9 %all-to-all-start.1 = ((bf16[128,2,1024]{2,1,0:T(2,128)(2,1)}), bf16[128,2,1024]{2,1,0:T(2,128)(2,1)S(1)}, u32[]{:S(2)}, u32[]{:S(2)}) async-start(bf16[128,2,1024]{2,1,0:T(2,128)(2,1)} %reshape.140), calls=%async_computation.1 | async-start | bytes 1048576 | tf_op jit(solution)/shard_map/all_to_all | solution.py:13
  35.5 43.0 %all-gather.4.cloned.1.call-start = ((), (), s32[]{:S(2)}) async-start(), calls=%async_computation.6 | async-start | bytes 2359296 | tf_op jit(solution)/shard_map/all_gather | solution.py:29
  51.6 96.4 %all-gather.6.cloned.1.call-start = ((), (), s32[]{:S(2)}) async-start(), calls=%async_computation.7 | async-start | bytes 2113536 | tf_op jit(solution)/shard_map/all_gather | solution.py:70
  54.8 18.3 %all-to-all-start.3 = ((bf16[128,2,1024]{2,1,0:T(2,128)(2,1)}), bf16[128,2,1024]{2,1,0:T(2,128)(2,1)S(1)}, u32[]{:S(2)}, u32[]{:S(2)}) async-start(bf16[128,2,1024]{2,1,0:T(2,128)(2,1)} %reshape.145), calls=%async_computation.3 | async-start | bytes 1048576 | tf_op jit(solution)/shard_map/all_to_all | solution.py:14
  59.4 115.3 %all-gather.8.cloned.1.call-start = ((), (), s32[]{:S(2)}) async-start(), calls=%async_computation.8 | async-start | bytes 2359296 | tf_op jit(solution)/shard_map/all_gather | solution.py:29
  78.5 2.4 copy-start
  81.4 68.8 %copy-start.1 = (bf16[128,1024]{1,0:T(8,128)(2,1)S(1)}, bf16[128,1024]{1,0:T(8,128)(2,1)}, u32[]{:S(2)}) copy-start(bf16[128,1024]{1,0:T(8,128)(2,1)} %scatter_custom_fusion.4) | copy-start | bytes 786436
  148.0 2.3 copy-start.3
  151.9 661.2 %reduce-scatter.2.cloned.1.call-start = ((), (), s32[]{:S(2)}) async-start(), calls=%async_computation.9 | async-start | bytes 4227072 | tf_op jit(solution)/shard_map/reduce_scatter | solution.py:80
  203.3 18.6 %all-to-all-start.2 = ((bf16[128,2,1024]{2,1,0:T(2,128)(2,1)}), bf16[128,2,1024]{2,1,0:T(2,128)(2,1)S(1)}, u32[]{:S(2)}, u32[]{:S(2)}) async-start(bf16[128,2,1024]{2,1,0:T(2,128)(2,1)} %get-tuple-element.4), calls=%async_computation.2 | async-start | bytes 1048576 | tf_op jit(solution)/shard_map/all_to_all | solution.py:21
Sparse Core Ops, SparseCore 0:
  51.7 26.7 all-gather.3
  81.6 66.2 all-gather.5
  152.0 22.5 all-gather.7
  176.9 636.1 reduce-scatter.1
where the time goes:
time: 828 us; the launch traced here: 821 us
  waiting for transfers between devices  722 us (87%)
  starting transfers between devices  25.5 us (3%)
  local copies, waits for them, and re-layouts  22.3 us (3%)
  blocking collectives  21.5 us (3%)
  between operations  14.7 us (2%)
  matrix products  8.82 us (1%)
    reduce_scatter x1, waiting for transfers between devices, per_device(): lax.psum_scatter(lax.dot_general(mixed_rows, grad_pre, (((0,), (0,)), (()...  589 us
    all_gather x1, waiting for transfers between devices, per_device(): whole_weight = lax.all_gather(weight, ('grp', 'in'), axis=0, tiled=True)  66.5 us
    all_to_all x1, blocking collectives, to_sources(): lax.all_to_all(grad_back, ('grp', 'in'), split_axis=0, concat_axis=0, til...  21.5 us
    all_gather x2, waiting for transfers between devices, propagate(): gathered = lax.all_gather(own_rows, 'in', axis=0, tiled=True)  21 us
  transfers between devices with their start and end apart: 8, of which 8 were waited for; matrix products, arithmetic and copies ran while one was open for 3% of the time, Pallas kernels for 0%

commit v1 on v0

v1 whole, which is shorter than its diff:
```python
import functools

import jax
import jax.numpy as jnp
from jax import lax
from jax.experimental import pallas as pl
from jax.experimental.pallas import tpu as pltpu
from jax.sharding import PartitionSpec as P

MESH = pl.DeviceIdType.MESH
BF = jnp.bfloat16
F32 = jnp.float32
I32 = jnp.int32

NG = 16
NI = 8
ROWS = 128
D = 1024
SLOTS = 256


def iota(shape, dim):
    return lax.broadcasted_iota(I32, shape, dim)


def ones_where(cond):
    return jnp.where(cond, 1.0, 0.0).astype(BF)


def dot(a, b):
    return jnp.dot(a, b, preferred_element_type=F32)


def dot_t0(a, b):
    return lax.dot_general(a, b, (((0,), (0,)), ((), ())), preferred_element_type=F32)


def dot_t1(a, b):
    return lax.dot_general(a, b, (((1,), (1,)), ((), ())), preferred_element_type=F32)


def kernel(
    cols_ref, count_ref, enc_ref, slot_ref, mask_ref, cot_ref, w_ref, val_ref,
    out_ref, grad_ref, wgrad_ref,
    s_rows, r_rows, s_pl, r_pl, s_cot, r_cot,
    w_f32, w_got, whole_w, adj,
    q_rows, x_slots, v_all, q_cot, c_slots, place,
    mixed, mixed_sib, mixed_rows,
    g_half, g_all, gf_out, gf_in,
    o_slots, o_mid, o_send, o_back,
    z_slots, z_mid, z_send, z_back,
    wg, wg_in, wg_sum, wg_out,
    rows_s, rows_r, pl_s, pl_r, cot_s, cot_r,
    w0_s, w0_r, w1_s, w1_r, w2_s, w2_r, w3_s, w3_r,
    a_s, a_r, f_s, f_r,
    x_s, x_r, v_s, v_r, c_s, c_r,
    m_s, m_r, ms_s, ms_r,
    g_s, g_r, gf_s, gf_r,
    o1_s, o1_r, o2_s, o2_r,
    z1_s, z1_r, z2_s, z2_r,
    rs_s, rs_r, t_s, t_r,
):
    mg = lax.axis_index("grp")
    mi = lax.axis_index("in")
    core = lax.rem(mi, 2)
    my_y = lax.div(mi, 2)
    sib = mi + 1 - 2 * core

    def grp_to(p):
        return lax.rem(mg + p, NG)

    def grp_from(p):
        return lax.rem(mg + NG - p, NG)

    def in_to(p):
        return lax.rem(mi + p, NI)

    def in_from(p):
        return lax.rem(mi + NI - p, NI)

    def rcopy(src, dst, ss, rs, dev):
        return pltpu.make_async_remote_copy(
            src_ref=src, dst_ref=dst, send_sem=ss, recv_sem=rs, device_id=dev, device_id_type=MESH
        )

    def got(dst, ss, rs):
        rcopy(dst, dst, ss, rs, (mg, sib)).wait_recv()

    def sent(src, ss, rs):
        rcopy(src, src, ss, rs, (mg, sib)).wait_send()

    def each(n, body):
        def step(p, carry):
            body(p)
            return carry

        lax.fori_loop(1, n, step, 0)

    t_grp = 4 * my_y + lax.div(mg, 4)
    t_in = 2 * lax.rem(mg, 4)
    from_grp = 4 * lax.rem(mg, 4) + my_y
    from_in = 2 * lax.div(mg, 4)
    half = core
    t_self = jnp.logical_and(t_grp == mg, lax.div(t_in, 2) == my_y)

    barrier = pltpu.get_barrier_semaphore()

    def greet(dev):
        pl.semaphore_signal(barrier, inc=1, device_id=dev, device_id_type=MESH)

    each(NG, lambda p: greet((grp_to(p), mi)))
    each(NI, lambda p: greet((mg, in_to(p))))
    for c in range(2):
        @pl.when(jnp.logical_not(jnp.logical_and(t_self, core == c)))
        def _():
            greet((from_grp, from_in + c))

    slot_row = slot_ref[...]
    eye = iota((ROWS, ROWS), 0) == iota((ROWS, ROWS), 1)
    slot_b = jnp.broadcast_to(slot_row, (ROWS, ROWS))
    slot_col = jnp.sum(jnp.where(eye, slot_b, 0), axis=1, keepdims=True)
    own_b = lax.shift_right_logical(slot_b, 7)
    own_col = lax.shift_right_logical(slot_col, 7)
    same = own_b == jnp.broadcast_to(own_col, (ROWS, ROWS))
    n_ix, m_ix = iota((ROWS, ROWS), 0), iota((ROWS, ROWS), 1)
    rank_row = jnp.sum(jnp.where(same & (n_ix < m_ix), 1, 0), axis=0, keepdims=True)
    rank_col = jnp.sum(jnp.where(same & (m_ix < n_ix), 1, 0), axis=1, keepdims=True)
    flat_row = lax.shift_right_logical(slot_row, 7) * 2 + rank_row
    flat_col = own_col * 2 + rank_col
    spread = iota((SLOTS, ROWS), 0) == jnp.broadcast_to(flat_row, (SLOTS, ROWS))
    collect = ones_where(
        iota((ROWS, SLOTS), 1) == jnp.broadcast_to(flat_col, (ROWS, SLOTS))
    )
    spread_rows = ones_where(spread)
    s_rows[...] = dot(spread_rows, enc_ref[...]).astype(BF).reshape(NG, 16, D)
    place1 = jnp.bitwise_and(slot_col, ROWS - 1) + 1
    place_b = jnp.broadcast_to(place1, (ROWS, ROWS)).astype(F32).astype(BF)
    s_pl[...] = dot(spread_rows, place_b).astype(BF).reshape(NG, 16, ROWS)

    n_send = jnp.where(t_self, 1, 2)
    pl.semaphore_wait(barrier, (NG - 1) + (NI - 1) + n_send)

    def grp_copy(src, dst, ss, rs):
        def go(p):
            rcopy(src.at[grp_to(p)], dst.at[mg], ss.at[p], rs.at[p], (grp_to(p), mi)).start()

        each(NG, go)

    def grp_got(dst, ss, rs):
        each(NG, lambda p: got(dst.at[grp_from(p)], ss.at[p], rs.at[p]))

    def grp_sent(src, ss, rs):
        each(NG, lambda p: sent(src.at[grp_to(p)], ss.at[p], rs.at[p]))

    def in_copy(src, dst, ss, rs):
        def go(p):
            rcopy(src(in_to(p)), dst(mi), ss.at[p], rs.at[p], (mg, in_to(p))).start()

        each(NI, go)

    def in_got(dst, ss, rs):
        each(NI, lambda p: got(dst(in_from(p)), ss.at[p], rs.at[p]))

    def in_sent(src, ss, rs):
        each(NI, lambda p: sent(src(in_to(p)), ss.at[p], rs.at[p]))

    grp_copy(s_pl, r_pl, pl_s, pl_r)
    grp_copy(s_rows, r_rows, rows_s, rows_r)
    r_pl[mg] = s_pl[mg]
    r_rows[mg] = s_rows[mg]

    w_f32[...] = w_ref[...].astype(F32)
    w0 = rcopy(w_f32, w_got, w0_s, w0_r, (mg, sib))
    w0.start()

    count = count_ref[0]
    for c in range(NI):
        acc = jnp.zeros((ROWS, ROWS), F32)
        for k in range(10):
            live = jnp.logical_and(cols_ref[0, k] == c, count > k)
            acc = acc + jnp.where(live, val_ref[k].astype(F32), 0.0)
        adj[mi, :, c * 128:(c + 1) * 128] = acc.astype(BF)
    rcopy(adj.at[mi], adj.at[mi], a_s.at[0], a_r.at[0], (mg, sib)).start()

    def y_to(q):
        return lax.rem(mi + 2 * q, NI)

    def y_from(q):
        return lax.rem(mi + NI - 2 * q, NI)

    def send_adj(q):
        rcopy(adj.at[mi], adj.at[mi], a_s.at[q], a_r.at[q], (mg, y_to(q))).start()

    each(4, send_adj)

    spread_cot = ones_where(spread & (jnp.broadcast_to(mask_ref[...], (SLOTS, ROWS)) > 0))
    s_cot[...] = dot(spread_cot, cot_ref[...]).astype(BF).reshape(NG, 16, D)
    grp_copy(s_cot, r_cot, cot_s, cot_r)
    r_cot[mg] = s_cot[mg]

    w0.wait()
    first = core == 0
    pair = jnp.concatenate(
        [
            jnp.where(first, w_f32[...], w_got[...]),
            jnp.where(first, w_got[...], w_f32[...]),
        ],
        axis=0,
    )
    pair = jnp.where(first, pair[:, :512], pair[:, 512:]).astype(BF)
    whole_w[core, mg * 4 + my_y] = pair

    def w1_copy(q):
        ref = whole_w.at[core, mg * 4 + my_y]
        rcopy(ref, ref, w1_s.at[q], w1_r.at[q], (mg, y_to(q))).start()

    each(4, w1_copy)

    r_ix, c_ix = iota((SLOTS, SLOTS), 0), iota((SLOTS, SLOTS), 1)

    def moved(ix):
        return (
            lax.shift_right_logical(jnp.bitwise_and(ix, 31), 1) * 16
            + lax.shift_right_logical(ix, 5) * 2
            + jnp.bitwise_and(ix, 1)
        )

    perm = ones_where(c_ix == moved(r_ix))
    perm_t = ones_where(r_ix == moved(c_ix))
    low = (jnp.bitwise_and(r_ix, 31) == jnp.bitwise_and(c_ix, 31)) & (
        lax.shift_right_logical(c_ix, 5) == mi
    )
    o_rows = ones_where(
        iota((16, SLOTS), 0) == lax.shift_right_logical(iota((16, SLOTS), 1), 5)
    )

    grp_got(r_pl, pl_s, pl_r)
    pl_cols = dot(perm, r_pl[...].reshape(SLOTS, ROWS))
    pl_wide = jnp.concatenate([pl_cols, pl_cols], axis=1)
    v_all[mi] = dot(o_rows, jnp.where(low, pl_wide, 0.0).astype(BF)).astype(BF)
    in_copy(lambda i: v_all.at[mi], lambda i: v_all.at[i], v_s, v_r)
    grp_got(r_rows, rows_s, rows_r)
    for f in range(NI):
        part = r_rows[:, :, f * 128:(f + 1) * 128].reshape(SLOTS, 128)
        q_rows[f] = dot(perm, part).astype(BF).reshape(NI, 32, 128)
    in_copy(lambda i: q_rows.at[i], lambda i: x_slots.at[:, i], x_s, x_r)
    x_slots[:, mi] = q_rows[mi]

    each(4, lambda q: got(whole_w.at[core, mg * 4 + y_from(q) // 2], w1_s.at[q], w1_r.at[q]))

    def w2_copy(p):
        ref = whole_w.at[core, pl.ds(mg * 4, 4)]
        rcopy(ref, ref, w2_s.at[p], w2_r.at[p], (grp_to(p), mi)).start()

    each(NG, w2_copy)

    def hand_on(q):
        ref = adj.at[y_from(q)]
        got(ref, a_s.at[q], a_r.at[q])
        rcopy(ref, ref, f_s.at[q], f_r.at[q], (mg, sib)).start()

    each(4, hand_on)

    grp_got(r_cot, cot_s, cot_r)
    q_cot[...] = dot(perm, r_cot[...].reshape(SLOTS, D)).astype(BF).reshape(NI, 32, D)
    in_copy(lambda i: q_cot.at[i], lambda i: c_slots.at[i], c_s, c_r)
    c_slots[mi] = q_cot[mi]

    in_got(lambda i: v_all.at[i], v_s, v_r)
    v_sum = v_all[0].astype(F32)
    for i in range(1, NI):
        v_sum = v_sum + v_all[i].astype(F32)
    node1 = (iota((ROWS, SLOTS), 0) + 1).astype(F32)
    for o in range(NI):
        place[o] = ones_where(node1 == jnp.broadcast_to(v_sum[o:o + 1, :], (ROWS, SLOTS)))

    got(adj.at[sib], a_s.at[0], a_r.at[0])
    each(4, lambda q: got(adj.at[lax.rem(sib + NI - 2 * q, NI)], f_s.at[q], f_r.at[q]))
    in_got(lambda i: x_slots.at[:, i], x_s, x_r)
    feats = jnp.concatenate(
        [dot(place[o], x_slots[o].reshape(SLOTS, 128)).astype(BF) for o in range(NI)], axis=0
    )
    for o in range(NI):
        mixed[o] = dot(adj[o], feats).astype(BF)
    in_copy(
        lambda i: mixed.at[i],
        lambda i: mixed_rows.at[:, pl.ds(pl.multiple_of(i * 128, 128), 128)],
        m_s, m_r,
    )
    ms = rcopy(mixed, mixed_sib, ms_s, ms_r, (mg, sib))
    ms.start()
    mixed_rows[:, pl.ds(pl.multiple_of(mi * 128, 128), 128)] = mixed[mi]

    each(NG, lambda p: got(whole_w.at[core, pl.ds(grp_from(p) * 4, 4)], w2_s.at[p], w2_r.at[p]))
    w3 = rcopy(whole_w.at[core], whole_w.at[core], w3_s, w3_r, (mg, sib))
    w3.start()

    in_got(lambda i: c_slots.at[i], c_s, c_r)
    own_cot = dot(place[mi], c_slots[...].reshape(SLOTS, D))

    got(whole_w.at[1 - core], w3_s, w3_r)
    in_got(
        lambda i: mixed_rows.at[:, pl.ds(pl.multiple_of(i * 128, 128), 128)], m_s, m_r
    )
    rows_val = mixed_rows[...]
    for h in range(2):
        v = dot(rows_val, whole_w[h].reshape(D, 512))
        k0 = 0.7978845608028654
        th = jnp.tanh(k0 * (v + 0.044715 * (v * v * v)))
        act = 0.5 * v * (1.0 + th)
        slope = 0.5 * (1.0 + th) + 0.5 * v * (1.0 - th * th) * (k0 * (1.0 + 3 * 0.044715 * (v * v)))
        o_mid_part = act.astype(BF)
        g_half[h] = (own_cot[:, h * 512:(h + 1) * 512] * slope).astype(BF)
        out_ref[:, h * 512:(h + 1) * 512] = o_mid_part

    for f in range(NI):
        w_rows = whole_w[:, f * 8:(f + 1) * 8]
        gf_out[f] = (
            dot_t1(g_half[0], w_rows[0].reshape(128, 512))
            + dot_t1(g_half[1], w_rows[1].reshape(128, 512))
        ).astype(BF)
    in_copy(lambda i: gf_out.at[i], lambda i: gf_in.at[i], gf_s, gf_r)
    gf_in[mi] = gf_out[mi]

    o_slots[...] = dot_t0(place[mi], out_ref[...]).astype(BF).reshape(NI, 32, D)
    in_copy(lambda i: o_slots.at[i], lambda i: o_mid.at[i], o1_s, o1_r)
    o_mid[mi] = o_slots[mi]

    in_copy(lambda i: g_half.at[lax.rem(i, 2)], lambda i: g_all.at[i], g_s, g_r)
    g_all[mi] = g_half[core]

    in_got(lambda i: gf_in.at[i], gf_s, gf_r)
    feed = gf_in[...].reshape(D, 128)
    for o in range(NI):
        back = dot(adj[o], feed).astype(BF)
        z_slots[:, o] = dot_t0(place[o], back).astype(BF).reshape(NI, 32, 128)
    in_copy(lambda i: z_slots.at[i], lambda i: z_mid.at[i], z1_s, z1_r)
    z_mid[mi] = z_slots[mi]

    in_got(lambda i: o_mid.at[i], o1_s, o1_r)
    o_send[...] = dot(perm_t, o_mid[...].reshape(SLOTS, D)).astype(BF).reshape(NG, 16, D)
    grp_copy(o_send, o_back, o2_s, o2_r)
    o_back[mg] = o_send[mg]

    in_got(lambda i: z_mid.at[i], z1_s, z1_r)
    for f in range(NI):
        z_send[:, :, f * 128:(f + 1) * 128] = (
            dot(perm_t, z_mid[f].reshape(SLOTS, 128)).astype(BF).reshape(NG, 16, 128)
        )
    grp_copy(z_send, z_back, z2_s, z2_r)
    z_back[mg] = z_send[mg]

    got(mixed_sib, ms_s, ms_r)
    in_got(lambda i: g_all.at[i], g_s, g_r)
    g_val = g_all[...].reshape(D, 512)
    mine = dot_t0(mixed[...].reshape(D, 128), g_val).reshape(8, 16, 512)
    other = dot_t0(mixed_sib[...].reshape(D, 128), g_val).reshape(8, 16, 512)
    wg[pl.ds(core * 8, 8)] = mine
    wg[pl.ds((1 - core) * 8, 8)] = other
    grp_copy(wg, wg_in, rs_s, rs_r)
    wg_in[mg] = wg[mg]
    grp_got(wg_in, rs_s, rs_r)
    total = wg_in[0]
    for g in range(1, NG):
        total = total + wg_in[g]
    total = total * (1.0 / 128)
    wg_sum[0] = total[:8]
    wg_sum[1] = total[8:]
    for h in range(2):
        @pl.when(jnp.logical_not(jnp.logical_and(t_self, core == h)))
        def _():
            rcopy(
                wg_sum.at[h], wg_out.at[core], t_s.at[h], t_r.at[core], (t_grp, t_in + h)
            ).start()

    @pl.when(t_self)
    def _():
        wg_out[core] = wg_sum[core]

    grp_got(o_back, o2_s, o2_r)
    out_ref[...] = dot(collect, o_back[...].reshape(SLOTS, D)).astype(BF)
    grp_got(z_back, z2_s, z2_r)
    grad_ref[...] = dot(collect, z_back[...].reshape(SLOTS, D)).astype(BF)

    for c in range(2):
        @pl.when(jnp.logical_not(jnp.logical_and(t_self, core == c)))
        def _():
            got(wg_out.at[c], t_s.at[c], t_r.at[c])
    wgrad_ref[:, :512] = wg_out[0]
    wgrad_ref[:, 512:] = wg_out[1]

    grp_sent(s_pl, pl_s, pl_r)
    grp_sent(s_rows, rows_s, rows_r)
    grp_sent(s_cot, cot_s, cot_r)
    sent(adj.at[mi], a_s.at[0], a_r.at[0])
    each(4, lambda q: sent(adj.at[mi], a_s.at[q], a_r.at[q]))
    each(4, lambda q: sent(adj.at[y_from(q)], f_s.at[q], f_r.at[q]))
    each(4, lambda q: sent(whole_w.at[core, mg * 4 + my_y], w1_s.at[q], w1_r.at[q]))
    each(NG, lambda p: sent(whole_w.at[core, pl.ds(mg * 4, 4)], w2_s.at[p], w2_r.at[p]))
    w3.wait_send()
    ms.wait_send()
    in_sent(lambda i: v_all.at[mi], v_s, v_r)
    in_sent(lambda i: q_rows.at[i], x_s, x_r)
    in_sent(lambda i: q_cot.at[i], c_s, c_r)
    in_sent(lambda i: mixed.at[i], m_s, m_r)
    in_sent(lambda i: gf_out.at[i], gf_s, gf_r)
    in_sent(lambda i: g_half.at[0], g_s, g_r)
    in_sent(lambda i: o_slots.at[i], o1_s, o1_r)
    in_sent(lambda i: z_slots.at[i], z1_s, z1_r)
    grp_sent(o_send, o2_s, o2_r)
    grp_sent(z_send, z2_s, z2_r)
    grp_sent(wg, rs_s, rs_r)
    for h in range(2):
        @pl.when(jnp.logical_not(jnp.logical_and(t_self, core == h)))
        def _():
            sent(wg_sum.at[h], t_s.at[h], t_r.at[core])


def scratch():
    v = pltpu.VMEM
    dma = pltpu.SemaphoreType.DMA
    grp_rows = v((NG, 16, D), BF)
    bufs = [
        grp_rows, grp_rows, v((NG, 16, ROWS), BF), v((NG, 16, ROWS), BF), grp_rows, grp_rows,
        v((8, D), F32), v((8, D), F32), v((2, 64, 16, 512), BF), v((NI, ROWS, D), BF),
        v((NI, NI, 32, 128), BF), v((NI, NI, 32, 128), BF), v((NI, 16, SLOTS), BF),
        v((NI, 32, D), BF), v((NI, 32, D), BF), v((NI, ROWS, SLOTS), BF),
        v((NI, ROWS, 128), BF), v((NI, ROWS, 128), BF), v((ROWS, D), BF),
        v((2, ROWS, 512), BF), v((NI, ROWS, 512), BF), v((NI, ROWS, 128), BF), v((NI, ROWS, 128), BF),
        v((NI, 32, D), BF), v((NI, 32, D), BF), grp_rows, grp_rows,
        v((NI, NI, 32, 128), BF), v((NI, NI, 32, 128), BF), grp_rows, grp_rows,
        v((NG, 16, 512), F32), v((NG, 16, 512), F32), v((2, 8, 512), F32), v((2, 8, 512), F32),
    ]
    g, i, y, one, two = dma((NG,)), dma((NI,)), dma((4,)), dma, dma((2,))
    sems = []
    for s in [g, g, g, one, y, g, one, y, y, i, i, i, i, one, i, i, i, g, i, g, g, two]:
        sems += [s, s]
    return bufs + sems


def per_device(
    encoded, owner_slot, label_mask, cotangent, weight, block_cols, block_counts, block_values
):
    vm = pl.BlockSpec(memory_space=pltpu.VMEM)
    sm = pl.BlockSpec(memory_space=pltpu.SMEM)
    return tuple(pl.pallas_call(
        kernel,
        out_shape=(
            jax.ShapeDtypeStruct((ROWS, D), BF),
            jax.ShapeDtypeStruct((ROWS, D), BF),
            jax.ShapeDtypeStruct((8, D), F32),
        ),
        in_specs=[sm, sm, vm, vm, vm, vm, vm, vm],
        out_specs=(vm, vm, vm),
        scratch_shapes=scratch(),
        compiler_params=pltpu.CompilerParams(
            collective_id=0, has_side_effects=True, vmem_limit_bytes=48 * 1024 * 1024
        ),
    )(
        block_cols, block_counts, encoded, owner_slot.reshape(1, ROWS),
        label_mask.reshape(1, ROWS), cotangent, weight, block_values[0],
    ))


def solution(mesh):
    rows = P(("grp", "in"), None)
    flat = P(("grp", "in"))
    in_specs = (rows, flat, flat, rows, rows, rows, flat, P(("grp", "in"), None, None, None))
    return jax.shard_map(
        per_device, mesh=mesh, in_specs=in_specs, out_specs=(rows, rows, rows), check_vma=False
    )
```

time: 828 us -> 99 us (0.12)
  the two profiles are of different devices: /device:TPU:1 before, /device:TPU:15 now
where the time goes in v1:
time: 99 us; the launch traced here: 98.7 us
  Pallas kernels  91.1 us (92%)
  local copies, waits for them, and re-layouts  6.27 us (6%)
  between operations  1.32 us (1%)
    pallas_call x1, Pallas kernels, per_device(): pl.pallas_call(kernel, out_shape=(jax.ShapeDtypeStruct((ROWS, D), BF), ja...  91.1 us
    unnamed x17, local copies, waits for them, and re-layouts  6.27 us

profile of v1, /device:TPU:15, one launch (start us, length us, event | category | flops | bytes accessed | tf_op | source)
XLA Modules:
  0.0 98.7 jit_solution(10960101171943173621)
XLA Ops:
  1.3 0.0 copy-start.4
  1.3 0.0 copy-start.5
  1.3 0.0 copy-start.6
  1.3 0.6 copy-done.4
  1.9 0.0 copy-done.5
  2.0 0.0 copy-done.6
  2.0 0.0 copy-start
  2.0 1.0 copy-done
  2.9 0.0 copy-start.1
  2.9 0.9 copy-done.1
  3.9 0.0 copy-start.2
  3.9 0.9 copy-done.2
  4.8 0.0 copy-start.3
  4.8 0.7 copy-done.3
  5.6 91.1 %shard_map.103 = (bf16[128,1024]{1,0:T(8,128)(2,1)S(1)}, bf16[128,1024]{1,0:T(8,128)(2,1)S(1)}, f32[8,1024]{1,0:T(8,128)S(1)}) custom-call(s32[1,10]{1,0:T(1,128)S(1)} %copy-done.4, s32[1]{0:T(128)S(6)} %copy.14.count_ref, bf16[128,1024]{1,0:T(8,128)(2,1)S(1)} %copy-done.1, s32[1,128]{1,0:T(1,128)S(1)} %bitcast.4, s32[1,128]{1,0:T(1,128)S(1)} %bitcast.5, ...), custom_call_target="tpu_custom_call" | custom-call | tf_op jit(solution)/shard_map/pallas_call | solution.py:446
  96.7 0.7 copy.15
  97.4 0.7 copy.16
  98.1 0.6 copy.17
Async XLA Ops:
  1.3 0.7 copy-start.4
  1.3 0.7 copy-start.5
  1.3 0.7 copy-start.6
  2.0 1.0 copy-start
  2.9 0.9 copy-start.1
  3.9 0.9 copy-start.2
  4.8 0.7 copy-start.3

commit v2 on v0

v2 whole, which is shorter than its diff:
```python
import functools

import jax
import jax.numpy as jnp
from jax import lax
from jax.experimental import pallas as pl
from jax.experimental.pallas import tpu as pltpu
from jax.sharding import PartitionSpec as P

MESH = pl.DeviceIdType.MESH
BF = jnp.bfloat16
F32 = jnp.float32
I32 = jnp.int32

NG = 16
NI = 8
ROWS = 128
D = 1024
SLOTS = 256


def iota(shape, dim):
    return lax.broadcasted_iota(I32, shape, dim)


def ones_where(cond):
    return jnp.where(cond, 1.0, 0.0).astype(BF)


def dot(a, b):
    return jnp.dot(a, b, preferred_element_type=F32)


def dot_t0(a, b):
    return lax.dot_general(a, b, (((0,), (0,)), ((), ())), preferred_element_type=F32)


def dot_t1(a, b):
    return lax.dot_general(a, b, (((1,), (1,)), ((), ())), preferred_element_type=F32)


def kernel(
    cols_ref, count_ref, slot_ref, mask_ref, enc_hbm, cot_hbm, w_hbm, val_hbm,
    out_ref, grad_ref, wgrad_ref,
    enc_ref, cot_ref, w_ref, val_ref,
    s_rows, r_rows, s_pl, r_pl, s_cot, r_cot,
    w_f32, w_got, whole_w, adj_up, adj,
    q_rows, x_slots, v_all, q_cot, c_slots, place, place_t,
    mixed, mixed_pair,
    g_half, g_pair, gf_out, gf_in,
    o_slots, o_mid, o_send, o_back,
    z_slots, z_mid, z_send, z_back,
    wa, wb, wa_in, wb_in, wa_sum, wb_sum, wa_in2, wb_in2, wy, wy_in, w_fin, w_fin_in,
    load,
    rows_s, rows_r, pl_s, pl_r, cot_s, cot_r,
    w0_s, w0_r, w1_s, w1_r, w2_s, w2_r, w3_s, w3_r,
    a_s, a_r, f_s, f_r,
    x_s, x_r, v_s, v_r, c_s, c_r,
    m_s, m_r, ms_s, ms_r,
    g_s, g_r, gf_s, gf_r,
    o1_s, o1_r, o2_s, o2_r,
    z1_s, z1_r, z2_s, z2_r,
    ra_s, ra_r, rb_s, rb_r, ra2_s, ra2_r, rb2_s, rb2_r, ry_s, ry_r, rf_s, rf_r,
):
    mg = lax.axis_index("grp")
    mi = lax.axis_index("in")
    core = lax.rem(mi, 2)
    my_y = lax.div(mi, 2)
    sib = mi + 1 - 2 * core

    arriving, leaving = {}, []

    def rcopy(src, dst, ss, rs, dev):
        return pltpu.make_async_remote_copy(
            src_ref=src, dst_ref=dst, send_sem=ss, recv_sem=rs, device_id=dev, device_id_type=MESH
        )

    def each(n, body):
        def step(p, carry):
            body(p)
            return carry

        lax.fori_loop(1, n, step, 0)

    def arrives(name, ref, rs):
        arriving[name] = lambda: rcopy(ref, ref, rs, rs, (mg, sib)).wait_recv()

    def leaves(ref, ss):
        leaving.append(lambda: rcopy(ref, ref, ss, ss, (mg, sib)).wait_send())

    def wait(name):
        arriving.pop(name)()

    def grp_to(p):
        return lax.rem(mg + p, NG)

    def in_to(p):
        return lax.rem(mi + p, NI)

    def y_to(q):
        return lax.rem(mi + 2 * q, NI)

    def y_from(q):
        return lax.rem(mi + NI - 2 * q, NI)

    def to_grp(name, src, dst, ss, rs):
        def go(p):
            rcopy(src.at[grp_to(p)], dst.at[mg], ss, rs, (grp_to(p), mi)).start()

        each(NG, go)
        leaves(src.at[pl.ds(0, NG - 1)], ss)
        arrives(name, dst.at[pl.ds(0, NG - 1)], rs)

    def to_in(name, src, dst, ss, rs, left, came):
        def go(p):
            rcopy(src(in_to(p)), dst, ss, rs, (mg, in_to(p))).start()

        each(NI, go)
        leaves(left, ss)
        arrives(name, came, rs)

    my_z, my_x = lax.div(mg, 4), lax.rem(mg, 4)

    def to_four(name, axis, src, dst, ss, rs, left, came):
        for q in range(1, 4):
            if axis == "x":
                n = lax.rem(my_x + q, 4)
                dev = (my_z * 4 + n, mi)
            elif axis == "z":
                n = lax.rem(my_z + q, 4)
                dev = (n * 4 + my_x, mi)
            else:
                n = lax.rem(my_y + q, 4)
                dev = (mg, n * 2 + core)
            rcopy(src(n), dst, ss, rs, dev).start()
        leaves(left, ss)
        arrives(name, came, rs)

    def to_sib(name, src, dst, ss, rs, came=None):
        rcopy(src, dst, ss, rs, (mg, sib)).start()
        leaves(src, ss)
        arrives(name, dst if came is None else came, rs)

    barrier = pltpu.get_barrier_semaphore()

    def greet(dev):
        pl.semaphore_signal(barrier, inc=1, device_id=dev, device_id_type=MESH)

    each(NG, lambda p: greet((grp_to(p), mi)))
    each(NI, lambda p: greet((mg, in_to(p))))

    loads = [
        pltpu.make_async_copy(src, dst, load.at[n])
        for n, (src, dst) in enumerate(
            [(enc_hbm, enc_ref), (w_hbm, w_ref), (val_hbm, val_ref), (cot_hbm, cot_ref)]
        )
    ]
    for copy in loads:
        copy.start()

    def body():
        slot_row = slot_ref[...]
        eye = iota((ROWS, ROWS), 0) == iota((ROWS, ROWS), 1)
        slot_b = jnp.broadcast_to(slot_row, (ROWS, ROWS))
        slot_col = jnp.sum(jnp.where(eye, slot_b, 0), axis=1, keepdims=True)
        own_b = lax.shift_right_logical(slot_b, 7)
        own_col = lax.shift_right_logical(slot_col, 7)
        same = own_b == jnp.broadcast_to(own_col, (ROWS, ROWS))
        n_ix, m_ix = iota((ROWS, ROWS), 0), iota((ROWS, ROWS), 1)
        rank_row = jnp.sum(jnp.where(same & (n_ix < m_ix), 1, 0), axis=0, keepdims=True)
        rank_col = jnp.sum(jnp.where(same & (m_ix < n_ix), 1, 0), axis=1, keepdims=True)
        flat_row = lax.shift_right_logical(slot_row, 7) * 2 + rank_row
        flat_col = own_col * 2 + rank_col
        spread = iota((SLOTS, ROWS), 0) == jnp.broadcast_to(flat_row, (SLOTS, ROWS))
        spread_rows = ones_where(spread)
        loads[0].wait()
        s_rows[...] = dot(spread_rows, enc_ref[...]).astype(BF).reshape(NG, 16, D)

        pl.semaphore_wait(barrier, (NG - 1) + (NI - 1))
        to_grp("rows", s_rows, r_rows, rows_s, rows_r)
        r_rows[mg] = s_rows[mg]

        place1 = jnp.bitwise_and(slot_col, ROWS - 1) + 1
        place_b = jnp.broadcast_to(place1, (ROWS, ROWS)).astype(F32).astype(BF)
        s_pl[...] = dot(spread_rows, place_b).astype(BF).reshape(NG, 16, ROWS)
        to_grp("pl", s_pl, r_pl, pl_s, pl_r)
        r_pl[mg] = s_pl[mg]
        loads[1].wait()
        w_f32[...] = w_ref[...].astype(F32)
        to_sib("w0", w_f32, w_got, w0_s, w0_r)

        loads[2].wait()
        count = count_ref[0, 0]
        for j in range(5):
            col = lax.rem(mi + j, NI)
            acc = jnp.zeros((ROWS, ROWS), F32)
            for k in range(10):
                live = jnp.logical_and(cols_ref[0, k] == col, count > k)
                acc = acc + val_ref[0, k].astype(F32) * jnp.where(live, 1.0, 0.0)
            adj_up[mi, j] = acc.astype(BF)
        wait("w0")
        first = core == 0
        pair = jnp.concatenate(
            [
                jnp.where(first, w_f32[...], w_got[...]),
                jnp.where(first, w_got[...], w_f32[...]),
            ],
            axis=0,
        )
        pair = jnp.where(first, pair[:, :512], pair[:, 512:]).astype(BF)
        mine_w = whole_w.at[core, my_z, my_x, my_y]
        mine_w[...] = pair
        to_four(
            "w1", "y", lambda n: mine_w, mine_w, w1_s, w1_r,
            whole_w.at[core, 0, 0, pl.ds(0, 3)], whole_w.at[core, 0, 0, pl.ds(0, 3)],
        )

        mine_up = adj_up.at[mi]
        for q in range(1, 4):
            rcopy(mine_up, mine_up, a_s.at[q], a_r.at[q], (mg, y_to(q))).start()
            leaves(mine_up, a_s.at[q])
            arrives("a%d" % q, mine_up, a_r.at[q])
        to_sib("a0", mine_up, mine_up, a_s.at[0], a_r.at[0])


        spread_cot = ones_where(spread & (jnp.broadcast_to(mask_ref[...], (SLOTS, ROWS)) > 0))
        loads[3].wait()
        s_cot[...] = dot(spread_cot, cot_ref[...]).astype(BF).reshape(NG, 16, D)
        to_grp("cot", s_cot, r_cot, cot_s, cot_r)
        r_cot[mg] = s_cot[mg]

        collect = ones_where(
            iota((ROWS, SLOTS), 1) == jnp.broadcast_to(flat_col, (ROWS, SLOTS))
        )
        flat_out = (
            jnp.bitwise_and(own_col, 7) * 32 + lax.shift_right_logical(own_col, 3) * 2 + rank_col
        )
        collect_out = ones_where(
            iota((ROWS, SLOTS), 1) == jnp.broadcast_to(flat_out, (ROWS, SLOTS))
        )

        r_ix, c_ix = iota((SLOTS, SLOTS), 0), iota((SLOTS, SLOTS), 1)

        def moved(ix):
            return (
                lax.shift_right_logical(jnp.bitwise_and(ix, 31), 1) * 16
                + lax.shift_right_logical(ix, 5) * 2
                + jnp.bitwise_and(ix, 1)
            )

        perm = ones_where(c_ix == moved(r_ix))
        perm_t = ones_where(r_ix == moved(c_ix))
        low = (jnp.bitwise_and(r_ix, 31) == jnp.bitwise_and(c_ix, 31)) & (
            lax.shift_right_logical(c_ix, 5) == mi
        )
        o_rows = ones_where(
            iota((16, SLOTS), 0) == lax.shift_right_logical(iota((16, SLOTS), 1), 5)
        )

        wait("pl")
        pl_cols = dot(perm, r_pl[...].reshape(SLOTS, ROWS))
        pl_wide = jnp.concatenate([pl_cols, pl_cols], axis=1)
        v_all[mi] = dot(o_rows, jnp.where(low, pl_wide, 0.0).astype(BF)).astype(BF)
        seven = pl.ds(0, NI - 1)
        to_in("v", lambda i: v_all.at[mi], v_all.at[mi], v_s, v_r, v_all.at[seven], v_all.at[seven])

        three, left_w, right_w = pl.ds(0, 3), pl.ds(0, 256), pl.ds(256, 256)
        wait("w1")
        group_l = whole_w.at[core, my_z, my_x, :, :, left_w]
        group_r = whole_w.at[core, my_z, my_x, :, :, right_w]
        some = whole_w.at[core, 0, three, :, :, left_w]
        to_four("w2l", "x", lambda n: group_l, group_l, w2_s.at[0], w2_r.at[0], some, some)
        to_four("w2r", "z", lambda n: group_r, group_r, w2_s.at[1], w2_r.at[1], some, some)
        wait("rows")
        for f in range(NI):
            part = r_rows[:, :, f * 128:(f + 1) * 128].reshape(SLOTS, 128)
            q_rows[f] = dot(perm, part).astype(BF).reshape(NI, 32, 128)
        to_in(
            "x", lambda i: q_rows.at[i], x_slots.at[:, mi], x_s, x_r,
            q_rows.at[seven], x_slots.at[:, seven],
        )
        x_slots[:, mi] = q_rows[mi]

        for q in range(1, 4):
            wait("a%d" % q)
            ref = adj_up.at[y_from(q)]
            to_sib(
                "f%d" % q, ref, ref, f_s.at[q], f_r.at[q],
                adj_up.at[lax.rem(sib + NI - 2 * q, NI)],
            )
        wait("cot")
        q_cot[...] = dot(perm, r_cot[...].reshape(SLOTS, D)).astype(BF).reshape(NI, 32, D)
        to_in(
            "c", lambda i: q_cot.at[i], c_slots.at[mi], c_s, c_r, q_cot.at[seven], c_slots.at[seven]
        )
        c_slots[mi] = q_cot[mi]

        wait("w2l")
        wait("w2r")
        plane_l = whole_w.at[core, my_z, :, :, :, left_w]
        plane_r = whole_w.at[core, :, my_x, :, :, right_w]
        some = whole_w.at[core, three, :, :, :, left_w]
        to_four("w3l", "z", lambda n: plane_l, plane_l, w2_s.at[2], w2_r.at[2], some, some)
        to_four("w3r", "x", lambda n: plane_r, plane_r, w2_s.at[3], w2_r.at[3], some, some)


        wait("v")
        v_sum = v_all[0].astype(F32)
        for i in range(1, NI):
            v_sum = v_sum + v_all[i].astype(F32)
        node1 = (iota((ROWS, SLOTS), 0) + 1).astype(F32)
        for o in range(NI):
            here = jnp.where(node1 == jnp.broadcast_to(v_sum[o:o + 1, :], (ROWS, SLOTS)), 1.0, 0.0)
            place[o] = here.astype(BF)
            place_t[o] = here.T.astype(BF)

        for name in ("a0", "f1", "f2", "f3"):
            wait(name)
        for r in range(NI):
            for j in range(5):
                c = (r + j) % NI
                adj[r * 128:(r + 1) * 128, c * 128:(c + 1) * 128] = adj_up[r, j]
                if 0 < j < 4:
                    flipped = adj_up[r, j].astype(F32).T.astype(BF)
                    adj[c * 128:(c + 1) * 128, r * 128:(r + 1) * 128] = flipped

        wait("x")
        feats = jnp.concatenate(
            [dot(place[o], x_slots[o].reshape(SLOTS, 128)).astype(BF) for o in range(NI)], axis=0
        )
        mixed[...] = dot(adj[...], feats).astype(BF).reshape(NI, ROWS, 128)
        my_rows = mixed_pair.at[0]
        my_cols = pl.ds(pl.multiple_of(mi * 128, 128), 128)
        to_in(
            "m", lambda i: mixed.at[i], my_rows.at[:, my_cols], m_s, m_r,
            mixed.at[seven], my_rows.at[:, pl.ds(0, 7 * 128)],
        )
        my_rows[:, my_cols] = mixed[mi]

        wait("w3l")
        wait("w3r")
        to_sib("w3", whole_w.at[core], whole_w.at[core], w3_s, w3_r, whole_w.at[1 - core])

        wait("c")
        place_out = dot(place[mi], perm).astype(BF)
        own_cot = dot(place[mi], c_slots[...].reshape(SLOTS, D))

        wait("w3")
        wait("m")
        to_sib("ms", my_rows, mixed_pair.at[1], ms_s, ms_r)
        rows_val = mixed_pair[0]
        for h in range(2):
            v = dot(rows_val, whole_w[h].reshape(D, 512))
            k0 = 0.7978845608028654
            th = jnp.tanh(k0 * (v + 0.044715 * (v * v * v)))
            act = 0.5 * v * (1.0 + th)
            slope = 0.5 * (1.0 + th) + 0.5 * v * (1.0 - th * th) * (k0 * (1.0 + 3 * 0.044715 * (v * v)))
            g_half[h] = (own_cot[:, h * 512:(h + 1) * 512] * slope).astype(BF)
            out_ref[:, h * 512:(h + 1) * 512] = act.astype(BF)

        to_sib("g", g_half.at[1 - core], g_pair.at[1], g_s, g_r)
        g_pair[0] = g_half[core]

        for f in range(NI):
            w_rows = whole_w[:, f // 2, f % 2 * 2:f % 2 * 2 + 2]
            gf_out[f] = (
                dot_t1(g_half[0], w_rows[0].reshape(128, 512))
                + dot_t1(g_half[1], w_rows[1].reshape(128, 512))
            ).astype(BF)
        to_in("gf", lambda i: gf_out.at[i], gf_in.at[mi], gf_s, gf_r, gf_out.at[seven], gf_in.at[seven])
        gf_in[mi] = gf_out[mi]

        o_slots[...] = dot_t0(place_out, out_ref[...]).astype(BF).reshape(NG, 16, D)
        to_grp("o1", o_slots, o_mid, o1_s, o1_r)
        o_mid[mg] = o_slots[mg]

        wait("ms")
        wait("g")
        m_val = mixed_pair[...].reshape(2 * ROWS, D)
        for h in range(2):
            term = dot_t0(m_val, g_pair[:, :, h * 256:(h + 1) * 256].reshape(2 * ROWS, 256))
            term = term.astype(BF).reshape(4, 4, 64, 256)
            for n in range(4):
                if h == 0:
                    wa[n] = term[:, n]
                else:
                    wb[n] = term[n]
        to_four("ra", "x", lambda n: wa.at[n], wa_in.at[my_x], ra_s, ra_r, wa.at[three], wa.at[three])
        to_four("rb", "z", lambda n: wb.at[n], wb_in.at[my_z], rb_s, rb_r, wb.at[three], wb.at[three])
        wa_in[my_x] = wa[my_x]
        wb_in[my_z] = wb[my_z]

        wait("gf")
        feed = gf_in[...].reshape(D, 128)
        back = dot(adj[...], feed).astype(BF)
        for o in range(NI):
            z_slots[:, o] = (
                dot(place_t[o], back[o * 128:(o + 1) * 128]).astype(BF).reshape(NI, 32, 128)
            )
        to_in("z1", lambda i: z_slots.at[i], z_mid.at[mi], z1_s, z1_r, z_slots.at[seven], z_mid.at[seven])
        z_mid[mi] = z_slots[mi]

        def add(ref):
            out = ref[0].astype(F32)
            for n in range(1, 4):
                out = out + ref[n].astype(F32)
            return out

        wait("ra")
        wa_sum[...] = add(wa_in).astype(BF)
        wait("rb")
        wb_sum[...] = add(wb_in).astype(BF)
        part = wa_sum.at[three]
        to_four("ra2", "z", lambda n: wa_sum.at[n], wa_in2.at[my_z], ra2_s, ra2_r, part, part)
        to_four("rb2", "x", lambda n: wb_sum.at[n], wb_in2.at[my_x], rb2_s, rb2_r, part, part)
        wa_in2[my_z] = wa_sum[my_z]
        wb_in2[my_x] = wb_sum[my_x]

        wait("z1")
        for f in range(NI):
            z_send[:, :, f * 128:(f + 1) * 128] = (
                dot(perm_t, z_mid[f].reshape(SLOTS, 128)).astype(BF).reshape(NG, 16, 128)
            )
        to_grp("z2", z_send, z_back, z2_s, z2_r)
        z_back[mg] = z_send[mg]

        wait("o1")
        o_send[...] = dot(perm, o_mid[...].reshape(SLOTS, D)).astype(BF).reshape(NI, 32, D)
        to_in("o2", lambda i: o_send.at[i], o_back.at[mi], o2_s, o2_r, o_send.at[seven], o_back.at[seven])
        o_back[mi] = o_send[mi]

        wait("ra2")
        wait("rb2")
        wy[:, :, :256] = add(wa_in2).reshape(4, 16, 256)
        wy[:, :, 256:] = add(wb_in2).reshape(4, 16, 256)
        to_four("ry", "y", lambda n: wy.at[n], wy_in.at[my_y], ry_s, ry_r, wy.at[three], wy.at[three])
        wy_in[my_y] = wy[my_y]
        wait("o2")
        out_ref[...] = dot(collect_out, o_back[...].reshape(SLOTS, D)).astype(BF)
        wait("ry")
        w_fin[...] = (add(wy_in) * (1.0 / 128)).reshape(2, 8, 512)
        to_sib("rf", w_fin.at[1 - core], w_fin_in, rf_s, rf_r)
        wgrad_ref[:, pl.ds(pl.multiple_of(core * 512, 512), 512)] = w_fin[core]
        wait("z2")
        grad_ref[...] = dot(collect, z_back[...].reshape(SLOTS, D)).astype(BF)
        wait("rf")
        wgrad_ref[:, pl.ds(pl.multiple_of((1 - core) * 512, 512), 512)] = w_fin_in[...]

    body()
    for name in list(arriving):
        wait(name)
    for done in leaving:
        done()


def store(a, b, c, a_out, b_out, c_out):
    a_out[...] = a[...]
    b_out[...] = b[...]
    c_out[...] = c[...]


def scratch():
    v = pltpu.VMEM
    dma = pltpu.SemaphoreType.DMA
    big, small = v((4, 4, 64, 256), BF), v((4, 64, 256), BF)
    grp_rows = v((NG, 16, D), BF)
    bufs = [
        v((ROWS, D), BF), v((ROWS, D), BF), v((8, D), BF), v((1, 10, ROWS, ROWS), BF),
        grp_rows, grp_rows, v((NG, 16, ROWS), BF), v((NG, 16, ROWS), BF), grp_rows, grp_rows,
        v((8, D), F32), v((8, D), F32), v((2, 4, 4, 4, 16, 512), BF), v((NI, 5, ROWS, ROWS), BF),
        v((D, D), BF),
        v((NI, NI, 32, 128), BF), v((NI, NI, 32, 128), BF), v((NI, 16, SLOTS), BF),
        v((NI, 32, D), BF), v((NI, 32, D), BF), v((NI, ROWS, SLOTS), BF), v((NI, SLOTS, ROWS), BF),
        v((NI, ROWS, 128), BF), v((2, ROWS, D), BF),
        v((2, ROWS, 512), BF), v((2, ROWS, 512), BF), v((NI, ROWS, 128), BF), v((NI, ROWS, 128), BF),
        grp_rows, grp_rows, v((NI, 32, D), BF), v((NI, 32, D), BF),
        v((NI, NI, 32, 128), BF), v((NI, NI, 32, 128), BF), grp_rows, grp_rows,
        big, big, big, big, small, small, small, small, v((4, 16, 512), F32), v((4, 16, 512), F32),
        v((2, 8, 512), F32), v((8, 512), F32),
    ]
    one, four = dma, dma((4,))
    sems = [four]
    for s in [one] * 5 + [four] + [one] + [four] * 2 + [one] * 17:
        sems += [s, s]
    return bufs + sems


def per_device(
    encoded, owner_slot, label_mask, cotangent, weight, block_cols, block_counts, block_values
):
    vm = pl.BlockSpec(memory_space=pltpu.VMEM)
    sm = pl.BlockSpec(memory_space=pltpu.SMEM)
    results = pl.pallas_call(
        kernel,
        out_shape=(
            jax.ShapeDtypeStruct((ROWS, D), BF),
            jax.ShapeDtypeStruct((ROWS, D), BF),
            jax.ShapeDtypeStruct((8, D), F32),
        ),
        in_specs=[sm, sm, vm, vm] + [pl.BlockSpec(memory_space=pl.ANY)] * 4,
        out_specs=(vm, vm, vm),
        scratch_shapes=scratch(),
        compiler_params=pltpu.CompilerParams(
            collective_id=0, has_side_effects=True, vmem_limit_bytes=60 * 1024 * 1024
        ),
    )(
        block_cols, block_counts.reshape(1, 1), owner_slot.reshape(1, ROWS), label_mask.reshape(1, ROWS),
        encoded, cotangent, weight, block_values,
    )
    return tuple(pl.pallas_call(
        store,
        out_shape=tuple(jax.ShapeDtypeStruct(r.shape, r.dtype) for r in results),
        in_specs=[vm] * 3,
        out_specs=(vm,) * 3,
    )(*results))


def solution(mesh):
    rows = P(("grp", "in"), None)
    flat = P(("grp", "in"))
    in_specs = (rows, flat, flat, rows, rows, rows, flat, P(("grp", "in"), None, None, None))
    return jax.shard_map(
        per_device, mesh=mesh, in_specs=in_specs, out_specs=(rows, rows, rows), check_vma=False
    )
```

time: 828 us -> 72 us (0.09)
  waiting for transfers between devices: 722 us -> 0 us
  Pallas kernels: 0 us -> 70.6 us
  starting transfers between devices: 25.5 us -> 0 us
  local copies, waits for them, and re-layouts: 22.3 us -> 0 us
  blocking collectives: 21.5 us -> 0 us
  between operations: 14.7 us -> 1.29 us
  matrix products: 8.82 us -> 0 us
    reduce_scatter x1 -> x0, waiting for transfers between devices: 589 us -> none  [per_device(): lax.psum_scatter(lax.dot_general(mixed_rows, grad_pre, (((0,), (0,)), (()...]
    all_gather x3 -> x0, waiting for transfers between devices: 87.6 us -> none  [the longest x1 66.5 us: per_device(): whole_weight = lax.all_gather(weight, ('grp', 'in'), axis=0, tiled=True)]
    pallas_call x0 -> x2, Pallas kernels: none -> 70.6 us  [the longest x1 68.7 us: per_device(): pl.pallas_call(kernel, out_shape=(jax.ShapeDtypeStruct((ROWS, D), BF), ja...]
    all_to_all x4 -> x0, waiting for transfers between devices: 43.8 us -> none  [the longest x1 12.9 us: to_owners(): lax.all_to_all(send_cot, ('grp', 'in'), split_axis=0, concat_axis=0, tile...]
    all_to_all x4 -> x0, starting transfers between devices: 25.2 us -> none  [the longest x1 11.5 us: to_owners(): lax.all_to_all(send_place, ('grp', 'in'), split_axis=0, concat_axis=0, ti...]
    all_to_all x1 -> x0, blocking collectives: 21.5 us -> none  [to_sources(): lax.all_to_all(grad_back, ('grp', 'in'), split_axis=0, concat_axis=0, til...]
    gather x8 -> x0, local copies, waits for them, and re-layouts: 10.5 us -> none  [the longest x2 4.65 us: propagate(): pieces = gathered.reshape(-1, block_size, feat_width)[block_cols]]
    dot_general x5 -> x0, matrix products: 8.82 us -> none  [the longest x1 2.83 us: per_device(): lax.dot_general(mixed_rows, grad_pre, (((0,), (0,)), ((), ())), preferred...]
  transfers between devices with their start and end apart: 8 -> 0, of which waited for: 8 -> 0; matrix products, arithmetic and copies ran while one was open for 3% -> 0% of each run, Pallas kernels for 0% -> 0%
where the time goes in v2:
time: 72 us; the launch traced here: 71.8 us
  Pallas kernels  70.6 us (98%)
  between operations  1.29 us (2%)
    pallas_call x1, Pallas kernels, per_device(): pl.pallas_call(kernel, out_shape=(jax.ShapeDtypeStruct((ROWS, D), BF), ja...  68.7 us
    pallas_call x1, Pallas kernels, per_device(): pl.pallas_call(store, out_shape=tuple((jax.ShapeDtypeStruct(r.shape, r.dt...  1.84 us

profile of v2, /device:TPU:1, one launch (start us, length us, event | category | flops | bytes accessed | tf_op | source)
XLA Modules:
  0.0 71.8 jit_solution(10807415571750525400)
XLA Ops:
  1.3 68.7 %shard_map.103 = (bf16[128,1024]{1,0:T(8,128)(2,1)}, bf16[128,1024]{1,0:T(8,128)(2,1)}, f32[8,1024]{1,0:T(8,128)}) custom-call(s32[1,10]{1,0:T(1,128)} %cols_ref.1, s32[1,1]{1,0:T(1,128)} %bitcast.3.count_ref, s32[1,128]{1,0:T(1,128)} %bitcast.4, s32[1,128]{1,0:T(1,128)} %bitcast.5, bf16[128,1024]{1,0:T(8,128)(2,1)} %enc_hbm.1, bf16[128,1024]{1,0:T(8,128)(2,1)} %cot_hbm.1, ...), custom_call_target="tpu_custom_call" | custom-call | tf_op jit(solution)/shard_map/pallas_call | solution.py:493
  70.0 1.8 %shard_map.104 = (bf16[128,1024]{1,0:T(8,128)(2,1)}, bf16[128,1024]{1,0:T(8,128)(2,1)}, f32[8,1024]{1,0:T(8,128)}) custom-call(bf16[128,1024]{1,0:T(8,128)(2,1)} %get-tuple-element.6.a, bf16[128,1024]{1,0:T(8,128)(2,1)} %get-tuple-element.7.b, f32[8,1024]{1,0:T(8,128)} %get-tuple-element.8.c), custom_call_target="tpu_custom_call" | custom-call | tf_op jit(solution)/shard_map/pallas_call | solution.py:510

commit v3 on v2

--- a/solution.py
+++ b/solution.py
@@ -40,9 +40,9 @@
 
 
 def kernel(
-    cols_ref, count_ref, slot_ref, mask_ref, enc_hbm, cot_hbm, w_hbm, val_hbm,
-    out_ref, grad_ref, wgrad_ref,
-    enc_ref, cot_ref, w_ref, val_ref,
+    cols_hbm, slot_hbm, mask_hbm, count_hbm, enc_hbm, cot_hbm, w_hbm, val_hbm,
+    out_hbm, grad_hbm, wgrad_hbm,
+    out_ref, grad_ref, wgrad_ref, cols_ref, slot_ref, mask_ref, count_ref, enc_ref, cot_ref, w_ref, val_ref,
     s_rows, r_rows, s_pl, r_pl, s_cot, r_cot,
     w_f32, w_got, whole_w, adj_up, adj,
     q_rows, x_slots, v_all, q_cot, c_slots, place, place_t,
@@ -50,8 +50,8 @@
     g_half, g_pair, gf_out, gf_in,
     o_slots, o_mid, o_send, o_back,
     z_slots, z_mid, z_send, z_back,
-    wa, wb, wa_in, wb_in, wa_sum, wb_sum, wa_in2, wb_in2, wy, wy_in, w_fin, w_fin_in,
-    load,
+    wa, wb, wa_in, wb_in, wa_sum, wb_sum, wa_in2, wb_in2, wy, wy_in,
+    load, store,
     rows_s, rows_r, pl_s, pl_r, cot_s, cot_r,
     w0_s, w0_r, w1_s, w1_r, w2_s, w2_r, w3_s, w3_r,
     a_s, a_r, f_s, f_r,
@@ -60,7 +60,7 @@
     g_s, g_r, gf_s, gf_r,
     o1_s, o1_r, o2_s, o2_r,
     z1_s, z1_r, z2_s, z2_r,
-    ra_s, ra_r, rb_s, rb_r, ra2_s, ra2_r, rb2_s, rb2_r, ry_s, ry_r, rf_s, rf_r,
+    ra_s, ra_r, rb_s, rb_r, ra2_s, ra2_r, rb2_s, rb2_r, ry_s, ry_r,
 ):
     mg = lax.axis_index("grp")
     mi = lax.axis_index("in")
@@ -92,10 +92,10 @@
         arriving.pop(name)()
 
     def grp_to(p):
-        return lax.rem(mg + p, NG)
+        return lax.rem(mg + 7 * p, NG)
 
     def in_to(p):
-        return lax.rem(mi + p, NI)
+        return lax.rem(mi + 3 * p, NI)
 
     def y_to(q):
         return lax.rem(mi + 2 * q, NI)
@@ -120,6 +120,7 @@
         arrives(name, came, rs)
 
     my_z, my_x = lax.div(mg, 4), lax.rem(mg, 4)
+    my_gz = lax.div(my_z, 2) * 4 + my_x
 
     def to_four(name, axis, src, dst, ss, rs, left, came):
         for q in range(1, 4):
@@ -141,24 +142,35 @@
         leaves(src, ss)
         arrives(name, dst if came is None else came, rs)
 
-    barrier = pltpu.get_barrier_semaphore()
-
-    def greet(dev):
-        pl.semaphore_signal(barrier, inc=1, device_id=dev, device_id_type=MESH)
-
-    each(NG, lambda p: greet((grp_to(p), mi)))
-    each(NI, lambda p: greet((mg, in_to(p))))
-
     loads = [
         pltpu.make_async_copy(src, dst, load.at[n])
         for n, (src, dst) in enumerate(
-            [(enc_hbm, enc_ref), (w_hbm, w_ref), (val_hbm, val_ref), (cot_hbm, cot_ref)]
+            [(enc_hbm, enc_ref), (w_hbm, w_ref), (val_hbm, val_ref), (cot_hbm, cot_ref), (count_hbm, count_ref),
+             (cols_hbm, cols_ref), (slot_hbm, slot_ref), (mask_hbm, mask_ref)]
         )
     ]
-    for copy in loads:
-        copy.start()
+    for n in (6, 0, 1, 2, 4, 5, 7, 3):
+        loads[n].start()
+
+    seven = pl.ds(0, NI - 1)
+
+    barrier = pltpu.get_barrier_semaphore()
+
+    def greet(dev):
+        pl.semaphore_signal(barrier, inc=1, device_id=dev, device_id_type=MESH)
+
+    each(NG, lambda p: greet((grp_to(p), mi)))
+    each(NI, lambda p: greet((mg, in_to(p))))
+
+    stores = [
+        pltpu.make_async_copy(src, dst, store.at[n])
+        for n, (src, dst) in enumerate(
+            [(out_ref, out_hbm), (grad_ref, grad_hbm), (wgrad_ref, wgrad_hbm)]
+        )
+    ]
 
     def body():
+        loads[6].wait()
         slot_row = slot_ref[...]
         eye = iota((ROWS, ROWS), 0) == iota((ROWS, ROWS), 1)
         slot_b = jnp.broadcast_to(slot_row, (ROWS, ROWS))
@@ -173,24 +185,26 @@
         flat_col = own_col * 2 + rank_col
         spread = iota((SLOTS, ROWS), 0) == jnp.broadcast_to(flat_row, (SLOTS, ROWS))
         spread_rows = ones_where(spread)
-        loads[0].wait()
-        s_rows[...] = dot(spread_rows, enc_ref[...]).astype(BF).reshape(NG, 16, D)
-
-        pl.semaphore_wait(barrier, (NG - 1) + (NI - 1))
-        to_grp("rows", s_rows, r_rows, rows_s, rows_r)
-        r_rows[mg] = s_rows[mg]
-
         place1 = jnp.bitwise_and(slot_col, ROWS - 1) + 1
         place_b = jnp.broadcast_to(place1, (ROWS, ROWS)).astype(F32).astype(BF)
         s_pl[...] = dot(spread_rows, place_b).astype(BF).reshape(NG, 16, ROWS)
+        loads[0].wait()
+        s_rows[...] = dot(spread_rows, enc_ref[...]).astype(BF).reshape(NG, 16, D)
+
+        pl.semaphore_wait(barrier, (NG - 1) + (NI - 1))
         to_grp("pl", s_pl, r_pl, pl_s, pl_r)
+        to_grp("rows", s_rows, r_rows, rows_s, rows_r)
+        r_rows[mg] = s_rows[mg]
+
         r_pl[mg] = s_pl[mg]
         loads[1].wait()
         w_f32[...] = w_ref[...].astype(F32)
         to_sib("w0", w_f32, w_got, w0_s, w0_r)
 
         loads[2].wait()
-        count = count_ref[0, 0]
+        loads[4].wait()
+        loads[5].wait()
+        count = count_ref[0]
         for j in range(5):
             col = lax.rem(mi + j, NI)
             acc = jnp.zeros((ROWS, ROWS), F32)
@@ -216,13 +230,14 @@
         )
 
         mine_up = adj_up.at[mi]
-        for q in range(1, 4):
+        for q in (1, 3):
             rcopy(mine_up, mine_up, a_s.at[q], a_r.at[q], (mg, y_to(q))).start()
             leaves(mine_up, a_s.at[q])
             arrives("a%d" % q, mine_up, a_r.at[q])
         to_sib("a0", mine_up, mine_up, a_s.at[0], a_r.at[0])
 
 
+        loads[7].wait()
         spread_cot = ones_where(spread & (jnp.broadcast_to(mask_ref[...], (SLOTS, ROWS)) > 0))
         loads[3].wait()
         s_cot[...] = dot(spread_cot, cot_ref[...]).astype(BF).reshape(NG, 16, D)
@@ -232,9 +247,13 @@
         collect = ones_where(
             iota((ROWS, SLOTS), 1) == jnp.broadcast_to(flat_col, (ROWS, SLOTS))
         )
-        flat_out = (
-            jnp.bitwise_and(own_col, 7) * 32 + lax.shift_right_logical(own_col, 3) * 2 + rank_col
-        )
+        own_g = lax.shift_right_logical(own_col, 3)
+        even_first = (
+            jnp.bitwise_and(own_g, 4) * 2
+            + lax.shift_right_logical(jnp.bitwise_and(own_g, 8), 1)
+            + jnp.bitwise_and(own_g, 3)
+        )
+        flat_out = jnp.bitwise_and(own_col, 7) * 32 + even_first * 2 + rank_col
         collect_out = ones_where(
             iota((ROWS, SLOTS), 1) == jnp.broadcast_to(flat_out, (ROWS, SLOTS))
         )
@@ -242,10 +261,12 @@
         r_ix, c_ix = iota((SLOTS, SLOTS), 0), iota((SLOTS, SLOTS), 1)
 
         def moved(ix):
+            z = jnp.bitwise_and(lax.shift_right_logical(ix, 2), 2) + jnp.bitwise_and(
+                lax.shift_right_logical(ix, 4), 1
+            )
+            x = jnp.bitwise_and(lax.shift_right_logical(ix, 1), 3)
             return (
-                lax.shift_right_logical(jnp.bitwise_and(ix, 31), 1) * 16
-                + lax.shift_right_logical(ix, 5) * 2
-                + jnp.bitwise_and(ix, 1)
+                (z * 4 + x) * 16 + lax.shift_right_logical(ix, 5) * 2 + jnp.bitwise_and(ix, 1)
             )
 
         perm = ones_where(c_ix == moved(r_ix))
@@ -261,7 +282,6 @@
         pl_cols = dot(perm, r_pl[...].reshape(SLOTS, ROWS))
         pl_wide = jnp.concatenate([pl_cols, pl_cols], axis=1)
         v_all[mi] = dot(o_rows, jnp.where(low, pl_wide, 0.0).astype(BF)).astype(BF)
-        seven = pl.ds(0, NI - 1)
         to_in("v", lambda i: v_all.at[mi], v_all.at[mi], v_s, v_r, v_all.at[seven], v_all.at[seven])
 
         three, left_w, right_w = pl.ds(0, 3), pl.ds(0, 256), pl.ds(256, 256)
@@ -271,6 +291,13 @@
         some = whole_w.at[core, 0, three, :, :, left_w]
         to_four("w2l", "x", lambda n: group_l, group_l, w2_s.at[0], w2_r.at[0], some, some)
         to_four("w2r", "z", lambda n: group_r, group_r, w2_s.at[1], w2_r.at[1], some, some)
+
+        for q, h in ((1, 2), (3, 4)):
+            wait("a%d" % q)
+            ref = adj_up.at[y_from(q), :, pl.ds(0 if q == 1 else 64, 64)]
+            rcopy(ref, ref, a_s.at[h], a_r.at[h], (mg, y_to(q))).start()
+            leaves(ref, a_s.at[h])
+            arrives("a%d" % h, ref, a_r.at[h])
         wait("rows")
         for f in range(NI):
             part = r_rows[:, :, f * 128:(f + 1) * 128].reshape(SLOTS, 128)
@@ -281,8 +308,9 @@
         )
         x_slots[:, mi] = q_rows[mi]
 
+        wait("a2")
+        wait("a4")
         for q in range(1, 4):
-            wait("a%d" % q)
             ref = adj_up.at[y_from(q)]
             to_sib(
                 "f%d" % q, ref, ref, f_s.at[q], f_r.at[q],
@@ -397,14 +425,25 @@
             z_slots[:, o] = (
                 dot(place_t[o], back[o * 128:(o + 1) * 128]).astype(BF).reshape(NI, 32, 128)
             )
-        to_in("z1", lambda i: z_slots.at[i], z_mid.at[mi], z1_s, z1_r, z_slots.at[seven], z_mid.at[seven])
+        for h in range(2):
+            rows_h = pl.ds(h * 16, 16)
+            to_in(
+                "z1%d" % h, lambda i: z_slots.at[i, :, rows_h], z_mid.at[mi, :, rows_h],
+                z1_s.at[h], z1_r.at[h], z_slots.at[seven, :, rows_h], z_mid.at[seven, :, rows_h],
+            )
         z_mid[mi] = z_slots[mi]
+
 
         def add(ref):
             out = ref[0].astype(F32)
             for n in range(1, 4):
                 out = out + ref[n].astype(F32)
             return out
+
+        wait("o1")
+        o_send[...] = dot(perm, o_mid[...].reshape(SLOTS, D)).astype(BF).reshape(NI, 32, D)
+        to_in("o2", lambda i: o_send.at[i], o_back.at[mi], o2_s, o2_r, o_send.at[seven], o_back.at[seven])
+        o_back[mi] = o_send[mi]
 
         wait("ra")
         wa_sum[...] = add(wa_in).astype(BF)
@@ -416,47 +455,74 @@
         wa_in2[my_z] = wa_sum[my_z]
         wb_in2[my_x] = wb_sum[my_x]
 
-        wait("z1")
-        for f in range(NI):
-            z_send[:, :, f * 128:(f + 1) * 128] = (
-                dot(perm_t, z_mid[f].reshape(SLOTS, 128)).astype(BF).reshape(NG, 16, 128)
-            )
-        to_grp("z2", z_send, z_back, z2_s, z2_r)
-        z_back[mg] = z_send[mg]
-
-        wait("o1")
-        o_send[...] = dot(perm, o_mid[...].reshape(SLOTS, D)).astype(BF).reshape(NI, 32, D)
-        to_in("o2", lambda i: o_send.at[i], o_back.at[mi], o2_s, o2_r, o_send.at[seven], o_back.at[seven])
-        o_back[mi] = o_send[mi]
+        pz_r, pz_c = iota((ROWS, ROWS), 0), iota((ROWS, ROWS), 1)
+        perm_z = ones_where(
+            pz_c == jnp.bitwise_and(lax.shift_right_logical(pz_r, 1), 7) * 16
+            + lax.shift_right_logical(pz_r, 4) * 2 + jnp.bitwise_and(pz_r, 1)
+        )
+        for h in range(2):
+            wait("z1%d" % h)
+            for f in range(NI):
+                z_send[h * 8:(h + 1) * 8, :, f * 128:(f + 1) * 128] = (
+                    dot(perm_z, z_mid[f, :, h * 16:(h + 1) * 16].reshape(ROWS, 128))
+                    .astype(BF).reshape(8, 16, 128)
+                )
+
+            def go(p, carry):
+                n = jnp.bitwise_and(my_gz + p, 7)
+                dest = lax.div(n, 4) * 8 + h * 4 + lax.rem(n, 4)
+
+                @pl.when(dest != mg)
+                def _():
+                    rcopy(z_send.at[h * 8 + n], z_back.at[mg], z2_s, z2_r, (dest, mi)).start()
+
+                return carry
+
+            lax.fori_loop(0, 8, go, 0)
+        leaves(z_send.at[pl.ds(0, NG - 1)], z2_s)
+        arrives("z2", z_back.at[pl.ds(0, NG - 1)], z2_r)
+        z_back[mg] = z_send[lax.rem(my_z, 2) * 8 + my_gz]
 
         wait("ra2")
         wait("rb2")
-        wy[:, :, :256] = add(wa_in2).reshape(4, 16, 256)
-        wy[:, :, 256:] = add(wb_in2).reshape(4, 16, 256)
-        to_four("ry", "y", lambda n: wy.at[n], wy_in.at[my_y], ry_s, ry_r, wy.at[three], wy.at[three])
-        wy_in[my_y] = wy[my_y]
+        wy[:, :, :256] = add(wa_in2).reshape(NI, 8, 256)
+        wy[:, :, 256:] = add(wb_in2).reshape(NI, 8, 256)
+        to_in("ry", lambda i: wy.at[i], wy_in.at[mi], ry_s, ry_r, wy.at[seven], wy_in.at[seven])
+        wy_in[mi] = wy[mi]
         wait("o2")
         out_ref[...] = dot(collect_out, o_back[...].reshape(SLOTS, D)).astype(BF)
+        stores[0].start()
         wait("ry")
-        w_fin[...] = (add(wy_in) * (1.0 / 128)).reshape(2, 8, 512)
-        to_sib("rf", w_fin.at[1 - core], w_fin_in, rf_s, rf_r)
-        wgrad_ref[:, pl.ds(pl.multiple_of(core * 512, 512), 512)] = w_fin[core]
+        for c in range(2):
+            half = wy_in[c]
+            for n in range(1, 4):
+                half = half + wy_in[2 * n + c]
+            wgrad_ref[:, c * 512:(c + 1) * 512] = half * (1.0 / 128)
+        stores[2].start()
         wait("z2")
         grad_ref[...] = dot(collect, z_back[...].reshape(SLOTS, D)).astype(BF)
-        wait("rf")
-        wgrad_ref[:, pl.ds(pl.multiple_of((1 - core) * 512, 512), 512)] = w_fin_in[...]
+        stores[1].start()
 
     body()
     for name in list(arriving):
         wait(name)
     for done in leaving:
         done()
-
-
-def store(a, b, c, a_out, b_out, c_out):
-    a_out[...] = a[...]
-    b_out[...] = b[...]
-    c_out[...] = c[...]
+    for copy in stores:
+        copy.wait()
+
+
+def hand_over(*refs):
+    here, out, kept, load, store = refs[:3], refs[3:6], refs[6:9], refs[9], refs[10]
+    loads = [pltpu.make_async_copy(here[n], kept[n], load.at[n]) for n in range(3)]
+    stores = [pltpu.make_async_copy(kept[n], out[n], store.at[n]) for n in range(3)]
+    for copy in loads:
+        copy.start()
+    for n in range(3):
+        loads[n].wait()
+        stores[n].start()
+    for copy in stores:
+        copy.wait()
 
 
 def scratch():
@@ -465,7 +531,8 @@
     big, small = v((4, 4, 64, 256), BF), v((4, 64, 256), BF)
     grp_rows = v((NG, 16, D), BF)
     bufs = [
-        v((ROWS, D), BF), v((ROWS, D), BF), v((8, D), BF), v((1, 10, ROWS, ROWS), BF),
+        v((ROWS, D), BF), v((ROWS, D), BF), v((8, D), F32), pltpu.SMEM((1, 10), I32),
+        v((1, ROWS), I32), v((1, ROWS), I32), pltpu.SMEM((1,), I32), v((ROWS, D), BF), v((ROWS, D), BF), v((8, D), BF), v((1, 10, ROWS, ROWS), BF),
         grp_rows, grp_rows, v((NG, 16, ROWS), BF), v((NG, 16, ROWS), BF), grp_rows, grp_rows,
         v((8, D), F32), v((8, D), F32), v((2, 4, 4, 4, 16, 512), BF), v((NI, 5, ROWS, ROWS), BF),
         v((D, D), BF),
@@ -475,12 +542,11 @@
         v((2, ROWS, 512), BF), v((2, ROWS, 512), BF), v((NI, ROWS, 128), BF), v((NI, ROWS, 128), BF),
         grp_rows, grp_rows, v((NI, 32, D), BF), v((NI, 32, D), BF),
         v((NI, NI, 32, 128), BF), v((NI, NI, 32, 128), BF), grp_rows, grp_rows,
-        big, big, big, big, small, small, small, small, v((4, 16, 512), F32), v((4, 16, 512), F32),
-        v((2, 8, 512), F32), v((8, 512), F32),
+        big, big, big, big, small, small, small, small, v((NI, 8, 512), F32), v((NI, 8, 512), F32),
     ]
-    one, four = dma, dma((4,))
-    sems = [four]
-    for s in [one] * 5 + [four] + [one] + [four] * 2 + [one] * 17:
+    one, two, four, five = dma, dma((2,)), dma((4,)), dma((5,))
+    sems = [dma((8,)), dma((3,))]
+    for s in [one] * 5 + [four] + [one] + [five, four] + [one] * 9 + [two] + [one] * 6:
         sems += [s, s]
     return bufs + sems
 
@@ -488,8 +554,7 @@
 def per_device(
     encoded, owner_slot, label_mask, cotangent, weight, block_cols, block_counts, block_values
 ):
-    vm = pl.BlockSpec(memory_space=pltpu.VMEM)
-    sm = pl.BlockSpec(memory_space=pltpu.SMEM)
+    anywhere = pl.BlockSpec(memory_space=pl.ANY)
     results = pl.pallas_call(
         kernel,
         out_shape=(
@@ -497,21 +562,23 @@
             jax.ShapeDtypeStruct((ROWS, D), BF),
             jax.ShapeDtypeStruct((8, D), F32),
         ),
-        in_specs=[sm, sm, vm, vm] + [pl.BlockSpec(memory_space=pl.ANY)] * 4,
-        out_specs=(vm, vm, vm),
+        in_specs=[anywhere] * 8,
+        out_specs=(anywhere,) * 3,
         scratch_shapes=scratch(),
         compiler_params=pltpu.CompilerParams(
             collective_id=0, has_side_effects=True, vmem_limit_bytes=60 * 1024 * 1024
         ),
     )(
-        block_cols, block_counts.reshape(1, 1), owner_slot.reshape(1, ROWS), label_mask.reshape(1, ROWS),
-        encoded, cotangent, weight, block_values,
+        block_cols, owner_slot.reshape(1, ROWS), label_mask.reshape(1, ROWS),
+        block_counts, encoded, cotangent, weight, block_values,
     )
     return tuple(pl.pallas_call(
-        store,
+        hand_over,
         out_shape=tuple(jax.ShapeDtypeStruct(r.shape, r.dtype) for r in results),
-        in_specs=[vm] * 3,
-        out_specs=(vm,) * 3,
+        in_specs=[anywhere] * 3,
+        out_specs=(anywhere,) * 3,
+        scratch_shapes=[pltpu.VMEM(r.shape, r.dtype) for r in results]
+        + [pltpu.SemaphoreType.DMA((3,))] * 2,
     )(*results))
 
 

time: 72 us -> 69.5 us (0.965)
  Pallas kernels: 70.6 us -> 68 us
    pallas_call x1, Pallas kernels: 68.7 us -> 66.2 us  [per_device(): pl.pallas_call(kernel, out_shape=(jax.ShapeDtypeStruct((ROWS, D), BF), ja...]
where the time goes in v3:
time: 69.5 us; the launch traced here: 69.3 us
  Pallas kernels  68 us (98%)
  between operations  1.29 us (2%)
    pallas_call x1, Pallas kernels, per_device(): pl.pallas_call(kernel, out_shape=(jax.ShapeDtypeStruct((ROWS, D), BF), ja...  66.2 us
    pallas_call x1, Pallas kernels, per_device(): pl.pallas_call(hand_over, out_shape=tuple((jax.ShapeDtypeStruct(r.shape,...  1.79 us

profile of v3, /device:TPU:1, one launch (start us, length us, event | category | flops | bytes accessed | tf_op | source)
XLA Modules:
  0.0 69.3 jit_solution(10935006532410315966)
XLA Ops:
  1.3 66.2 %shard_map.103 = (bf16[128,1024]{1,0:T(8,128)(2,1)}, bf16[128,1024]{1,0:T(8,128)(2,1)}, f32[8,1024]{1,0:T(8,128)}) custom-call(s32[1,10]{1,0:T(1,128)} %cols_hbm.1, s32[1,128]{1,0:T(1,128)} %bitcast.2, s32[1,128]{1,0:T(1,128)} %bitcast.3, s32[1]{0:T(128)S(6)} %copy.11.count_hbm, bf16[128,1024]{1,0:T(8,128)(2,1)} %enc_hbm.1, bf16[128,1024]{1,0:T(8,128)(2,1)} %cot_hbm.1, ...), custom_call_target="tpu_custom_call" | custom-call | tf_op jit(solution)/shard_map/pallas_call | solution.py:558
  67.5 1.8 %shard_map.104 = (bf16[128,1024]{1,0:T(8,128)(2,1)}, bf16[128,1024]{1,0:T(8,128)(2,1)}, f32[8,1024]{1,0:T(8,128)}) custom-call(bf16[128,1024]{1,0:T(8,128)(2,1)} %get-tuple-element.6.refs_0_, bf16[128,1024]{1,0:T(8,128)(2,1)} %get-tuple-element.7.refs_1_, f32[8,1024]{1,0:T(8,128)} %get-tuple-element.8.refs_2_), custom_call_target="tpu_custom_call" | custom-call | tf_op jit(solution)/shard_map/pallas_call | solution.py:575

commit v4 on v3

--- a/solution.py
+++ b/solution.py
@@ -41,17 +41,18 @@
 
 def kernel(
     cols_hbm, slot_hbm, mask_hbm, count_hbm, enc_hbm, cot_hbm, w_hbm, val_hbm,
-    out_hbm, grad_hbm, wgrad_hbm,
-    out_ref, grad_ref, wgrad_ref, cols_ref, slot_ref, mask_ref, count_ref, enc_ref, cot_ref, w_ref, val_ref,
-    s_rows, r_rows, s_pl, r_pl, s_cot, r_cot,
+    out_ref, grad_ref, wgrad_ref,
+    cols_ref, slot_ref, mask_ref, count_ref, enc_ref, cot_ref, w_ref, val_ref,
+    s_rows, r_rows, s_pl, r_pl, s_cot, r_cot, s_cot2, r_cot2,
     w_f32, w_got, whole_w, adj_up, adj,
-    q_rows, x_slots, v_all, q_cot, c_slots, place, place_t,
+    q_rows, x_slots, v_all, q_cot, c_slots, q_cot2, c_slots2, place, place_t,
     mixed, mixed_pair,
     g_half, g_pair, gf_out, gf_in,
     o_slots, o_mid, o_send, o_back,
+    p_slots, p_mid, p_send, p_back,
     z_slots, z_mid, z_send, z_back,
     wa, wb, wa_in, wb_in, wa_sum, wb_sum, wa_in2, wb_in2, wy, wy_in,
-    load, store,
+    load,
     rows_s, rows_r, pl_s, pl_r, cot_s, cot_r,
     w0_s, w0_r, w1_s, w1_r, w2_s, w2_r, w3_s, w3_r,
     a_s, a_r, f_s, f_r,
@@ -61,6 +62,7 @@
     o1_s, o1_r, o2_s, o2_r,
     z1_s, z1_r, z2_s, z2_r,
     ra_s, ra_r, rb_s, rb_r, ra2_s, ra2_r, rb2_s, rb2_r, ry_s, ry_r,
+    cot2_s, cot2_r, c2_s, c2_r, p1_s, p1_r, p2_s, p2_r,
 ):
     mg = lax.axis_index("grp")
     mi = lax.axis_index("in")
@@ -161,13 +163,6 @@
 
     each(NG, lambda p: greet((grp_to(p), mi)))
     each(NI, lambda p: greet((mg, in_to(p))))
-
-    stores = [
-        pltpu.make_async_copy(src, dst, store.at[n])
-        for n, (src, dst) in enumerate(
-            [(out_ref, out_hbm), (grad_ref, grad_hbm), (wgrad_ref, wgrad_hbm)]
-        )
-    ]
 
     def body():
         loads[6].wait()
@@ -238,22 +233,43 @@
 
 
         loads[7].wait()
-        spread_cot = ones_where(spread & (jnp.broadcast_to(mask_ref[...], (SLOTS, ROWS)) > 0))
+        labelled = mask_ref[...] > 0
+        spread_cot = ones_where(spread & jnp.broadcast_to(labelled, (SLOTS, ROWS)))
+
+        def even_first(g):
+            return (
+                jnp.bitwise_and(g, 4) * 2
+                + lax.shift_right_logical(jnp.bitwise_and(g, 8), 1)
+                + jnp.bitwise_and(g, 3)
+            )
+
+        own_row = lax.shift_right_logical(slot_row, 7)
+        flat_in = (
+            jnp.bitwise_and(own_row, 7) * 32
+            + even_first(lax.shift_right_logical(own_row, 3)) * 2 + rank_row
+        )
+        spread_in = ones_where(
+            iota((SLOTS, ROWS), 0)
+            == jnp.broadcast_to(jnp.where(labelled, flat_in, -1), (SLOTS, ROWS))
+        )
         loads[3].wait()
-        s_cot[...] = dot(spread_cot, cot_ref[...]).astype(BF).reshape(NG, 16, D)
+        s_cot2[...] = dot(spread_in, cot_ref[:, 512:]).astype(BF).reshape(NI, 32, 512)
+        to_in(
+            "cot2", lambda i: s_cot2.at[i], r_cot2.at[mi], cot2_s, cot2_r,
+            s_cot2.at[seven], r_cot2.at[seven],
+        )
+        r_cot2[mi] = s_cot2[mi]
+        s_cot[...] = dot(spread_cot, cot_ref[:, :512]).astype(BF).reshape(NG, 16, 512)
         to_grp("cot", s_cot, r_cot, cot_s, cot_r)
         r_cot[mg] = s_cot[mg]
 
         collect = ones_where(
             iota((ROWS, SLOTS), 1) == jnp.broadcast_to(flat_col, (ROWS, SLOTS))
         )
-        own_g = lax.shift_right_logical(own_col, 3)
-        even_first = (
-            jnp.bitwise_and(own_g, 4) * 2
-            + lax.shift_right_logical(jnp.bitwise_and(own_g, 8), 1)
-            + jnp.bitwise_and(own_g, 3)
-        )
-        flat_out = jnp.bitwise_and(own_col, 7) * 32 + even_first * 2 + rank_col
+        flat_out = (
+            jnp.bitwise_and(own_col, 7) * 32
+            + even_first(lax.shift_right_logical(own_col, 3)) * 2 + rank_col
+        )
         collect_out = ones_where(
             iota((ROWS, SLOTS), 1) == jnp.broadcast_to(flat_out, (ROWS, SLOTS))
         )
@@ -317,7 +333,7 @@
                 adj_up.at[lax.rem(sib + NI - 2 * q, NI)],
             )
         wait("cot")
-        q_cot[...] = dot(perm, r_cot[...].reshape(SLOTS, D)).astype(BF).reshape(NI, 32, D)
+        q_cot[...] = dot(perm, r_cot[...].reshape(SLOTS, 512)).astype(BF).reshape(NI, 32, 512)
         to_in(
             "c", lambda i: q_cot.at[i], c_slots.at[mi], c_s, c_r, q_cot.at[seven], c_slots.at[seven]
         )
@@ -331,6 +347,11 @@
         to_four("w3l", "z", lambda n: plane_l, plane_l, w2_s.at[2], w2_r.at[2], some, some)
         to_four("w3r", "x", lambda n: plane_r, plane_r, w2_s.at[3], w2_r.at[3], some, some)
 
+
+        wait("cot2")
+        q_cot2[...] = dot(perm_t, r_cot2[...].reshape(SLOTS, 512)).astype(BF).reshape(NG, 16, 512)
+        to_grp("c2", q_cot2, c_slots2, c2_s, c2_r)
+        c_slots2[mg] = q_cot2[mg]
 
         wait("v")
         v_sum = v_all[0].astype(F32)
@@ -371,7 +392,11 @@
 
         wait("c")
         place_out = dot(place[mi], perm).astype(BF)
-        own_cot = dot(place[mi], c_slots[...].reshape(SLOTS, D))
+        wait("c2")
+        own_cot = (
+            dot(place[mi], c_slots[...].reshape(SLOTS, 512)),
+            dot(place_out, c_slots2[...].reshape(SLOTS, 512)),
+        )
 
         wait("w3")
         wait("m")
@@ -383,7 +408,7 @@
             th = jnp.tanh(k0 * (v + 0.044715 * (v * v * v)))
             act = 0.5 * v * (1.0 + th)
             slope = 0.5 * (1.0 + th) + 0.5 * v * (1.0 - th * th) * (k0 * (1.0 + 3 * 0.044715 * (v * v)))
-            g_half[h] = (own_cot[:, h * 512:(h + 1) * 512] * slope).astype(BF)
+            g_half[h] = (own_cot[h] * slope).astype(BF)
             out_ref[:, h * 512:(h + 1) * 512] = act.astype(BF)
 
         to_sib("g", g_half.at[1 - core], g_pair.at[1], g_s, g_r)
@@ -398,9 +423,12 @@
         to_in("gf", lambda i: gf_out.at[i], gf_in.at[mi], gf_s, gf_r, gf_out.at[seven], gf_in.at[seven])
         gf_in[mi] = gf_out[mi]
 
-        o_slots[...] = dot_t0(place_out, out_ref[...]).astype(BF).reshape(NG, 16, D)
+        o_slots[...] = dot_t0(place_out, out_ref[:, :512]).astype(BF).reshape(NG, 16, 512)
         to_grp("o1", o_slots, o_mid, o1_s, o1_r)
         o_mid[mg] = o_slots[mg]
+        p_slots[...] = dot_t0(place[mi], out_ref[:, 512:]).astype(BF).reshape(NI, 32, 512)
+        to_in("p1", lambda i: p_slots.at[i], p_mid.at[mi], p1_s, p1_r, p_slots.at[seven], p_mid.at[seven])
+        p_mid[mi] = p_slots[mi]
 
         wait("ms")
         wait("g")
@@ -440,8 +468,13 @@
                 out = out + ref[n].astype(F32)
             return out
 
+        wait("p1")
+        p_send[...] = dot(perm_t, p_mid[...].reshape(SLOTS, 512)).astype(BF).reshape(NG, 16, 512)
+        to_grp("p2", p_send, p_back, p2_s, p2_r)
+        p_back[mg] = p_send[mg]
+
         wait("o1")
-        o_send[...] = dot(perm, o_mid[...].reshape(SLOTS, D)).astype(BF).reshape(NI, 32, D)
+        o_send[...] = dot(perm, o_mid[...].reshape(SLOTS, 512)).astype(BF).reshape(NI, 32, 512)
         to_in("o2", lambda i: o_send.at[i], o_back.at[mi], o2_s, o2_r, o_send.at[seven], o_back.at[seven])
         o_back[mi] = o_send[mi]
 
@@ -490,38 +523,33 @@
         to_in("ry", lambda i: wy.at[i], wy_in.at[mi], ry_s, ry_r, wy.at[seven], wy_in.at[seven])
         wy_in[mi] = wy[mi]
         wait("o2")
-        out_ref[...] = dot(collect_out, o_back[...].reshape(SLOTS, D)).astype(BF)
-        stores[0].start()
+        out_ref[:, :512] = dot(collect_out, o_back[...].reshape(SLOTS, 512)).astype(BF)
+        wait("p2")
+        out_ref[:, 512:] = dot(collect, p_back[...].reshape(SLOTS, 512)).astype(BF)
         wait("ry")
         for c in range(2):
             half = wy_in[c]
             for n in range(1, 4):
                 half = half + wy_in[2 * n + c]
             wgrad_ref[:, c * 512:(c + 1) * 512] = half * (1.0 / 128)
-        stores[2].start()
         wait("z2")
         grad_ref[...] = dot(collect, z_back[...].reshape(SLOTS, D)).astype(BF)
-        stores[1].start()
 
     body()
     for name in list(arriving):
         wait(name)
     for done in leaving:
         done()
-    for copy in stores:
-        copy.wait()
-
-
-def hand_over(*refs):
-    here, out, kept, load, store = refs[:3], refs[3:6], refs[6:9], refs[9], refs[10]
-    loads = [pltpu.make_async_copy(here[n], kept[n], load.at[n]) for n in range(3)]
-    stores = [pltpu.make_async_copy(kept[n], out[n], store.at[n]) for n in range(3)]
-    for copy in loads:
+
+
+def hand_over(a, b, c, a_out, b_out, c_out, sem):
+    copies = [
+        pltpu.make_async_copy(src, dst, sem.at[n])
+        for n, (src, dst) in enumerate([(a, a_out), (b, b_out), (c, c_out)])
+    ]
+    for copy in copies:
         copy.start()
-    for n in range(3):
-        loads[n].wait()
-        stores[n].start()
-    for copy in stores:
+    for copy in copies:
         copy.wait()
 
 
@@ -530,23 +558,25 @@
     dma = pltpu.SemaphoreType.DMA
     big, small = v((4, 4, 64, 256), BF), v((4, 64, 256), BF)
     grp_rows = v((NG, 16, D), BF)
+    grp_half, in_half = v((NG, 16, 512), BF), v((NI, 32, 512), BF)
     bufs = [
-        v((ROWS, D), BF), v((ROWS, D), BF), v((8, D), F32), pltpu.SMEM((1, 10), I32),
+        pltpu.SMEM((1, 10), I32),
         v((1, ROWS), I32), v((1, ROWS), I32), pltpu.SMEM((1,), I32), v((ROWS, D), BF), v((ROWS, D), BF), v((8, D), BF), v((1, 10, ROWS, ROWS), BF),
-        grp_rows, grp_rows, v((NG, 16, ROWS), BF), v((NG, 16, ROWS), BF), grp_rows, grp_rows,
+        grp_rows, grp_rows, v((NG, 16, ROWS), BF), v((NG, 16, ROWS), BF),
+        grp_half, grp_half, in_half, in_half,
         v((8, D), F32), v((8, D), F32), v((2, 4, 4, 4, 16, 512), BF), v((NI, 5, ROWS, ROWS), BF),
         v((D, D), BF),
         v((NI, NI, 32, 128), BF), v((NI, NI, 32, 128), BF), v((NI, 16, SLOTS), BF),
-        v((NI, 32, D), BF), v((NI, 32, D), BF), v((NI, ROWS, SLOTS), BF), v((NI, SLOTS, ROWS), BF),
+        in_half, in_half, grp_half, grp_half, v((NI, ROWS, SLOTS), BF), v((NI, SLOTS, ROWS), BF),
         v((NI, ROWS, 128), BF), v((2, ROWS, D), BF),
         v((2, ROWS, 512), BF), v((2, ROWS, 512), BF), v((NI, ROWS, 128), BF), v((NI, ROWS, 128), BF),
-        grp_rows, grp_rows, v((NI, 32, D), BF), v((NI, 32, D), BF),
+        grp_half, grp_half, in_half, in_half, in_half, in_half, grp_half, grp_half,
         v((NI, NI, 32, 128), BF), v((NI, NI, 32, 128), BF), grp_rows, grp_rows,
         big, big, big, big, small, small, small, small, v((NI, 8, 512), F32), v((NI, 8, 512), F32),
     ]
     one, two, four, five = dma, dma((2,)), dma((4,)), dma((5,))
-    sems = [dma((8,)), dma((3,))]
-    for s in [one] * 5 + [four] + [one] + [five, four] + [one] * 9 + [two] + [one] * 6:
+    sems = [dma((8,))]
+    for s in [one] * 5 + [four] + [one] + [five, four] + [one] * 9 + [two] + [one] * 10:
         sems += [s, s]
     return bufs + sems
 
@@ -555,18 +585,17 @@
     encoded, owner_slot, label_mask, cotangent, weight, block_cols, block_counts, block_values
 ):
     anywhere = pl.BlockSpec(memory_space=pl.ANY)
+    vm = pl.BlockSpec(memory_space=pltpu.VMEM)
     results = pl.pallas_call(
         kernel,
         out_shape=(
-            jax.ShapeDtypeStruct((ROWS, D), BF),
-            jax.ShapeDtypeStruct((ROWS, D), BF),
-            jax.ShapeDtypeStruct((8, D), F32),
+            pltpu.VMEM((ROWS, D), BF), pltpu.VMEM((ROWS, D), BF), pltpu.VMEM((8, D), F32),
         ),
         in_specs=[anywhere] * 8,
-        out_specs=(anywhere,) * 3,
+        out_specs=(vm,) * 3,
         scratch_shapes=scratch(),
         compiler_params=pltpu.CompilerParams(
-            collective_id=0, has_side_effects=True, vmem_limit_bytes=60 * 1024 * 1024
+            collective_id=0, has_side_effects=True, vmem_limit_bytes=58 * 1024 * 1024
         ),
     )(
         block_cols, owner_slot.reshape(1, ROWS), label_mask.reshape(1, ROWS),
@@ -575,11 +604,10 @@
     return tuple(pl.pallas_call(
         hand_over,
         out_shape=tuple(jax.ShapeDtypeStruct(r.shape, r.dtype) for r in results),
-        in_specs=[anywhere] * 3,
+        in_specs=[vm] * 3,
         out_specs=(anywhere,) * 3,
-        scratch_shapes=[pltpu.VMEM(r.shape, r.dtype) for r in results]
-        + [pltpu.SemaphoreType.DMA((3,))] * 2,
-    )(*results))
+        scratch_shapes=[pltpu.SemaphoreType.DMA((3,))],
+    )(*[pltpu.with_memory_space_constraint(r, pltpu.VMEM) for r in results]))
 
 
 def solution(mesh):

time: 69.5 us -> 64.9 us (0.934)
  the two profiles are of different devices: /device:TPU:1 before, /device:TPU:3 now
where the time goes in v4:
time: 64.9 us; the launch traced here: 64.8 us
  Pallas kernels  63.5 us (98%)
  between operations  1.29 us (2%)
    pallas_call x1, Pallas kernels, per_device(): pl.pallas_call(kernel, out_shape=(pltpu.VMEM((ROWS, D), BF), pltpu.VMEM((...  62.7 us

profile of v4, /device:TPU:3, one launch (start us, length us, event | category | flops | bytes accessed | tf_op | source)
XLA Modules:
  0.0 64.8 jit_solution(18103407410485899406)
XLA Ops:
  1.3 62.7 %shard_map.103 = (bf16[128,1024]{1,0:T(8,128)(2,1)S(1)}, bf16[128,1024]{1,0:T(8,128)(2,1)S(1)}, f32[8,1024]{1,0:T(8,128)S(1)}) custom-call(s32[1,10]{1,0:T(1,128)} %cols_hbm.1, s32[1,128]{1,0:T(1,128)} %bitcast.2, s32[1,128]{1,0:T(1,128)} %bitcast.3, s32[1]{0:T(128)S(6)} %copy.11.count_hbm, bf16[128,1024]{1,0:T(8,128)(2,1)} %enc_hbm.1, ...), custom_call_target="tpu_custom_call" | custom-call | tf_op jit(solution)/shard_map/pallas_call | solution.py:589
  64.0 0.8 %shard_map.104 = (bf16[128,1024]{1,0:T(8,128)(2,1)}, bf16[128,1024]{1,0:T(8,128)(2,1)}, f32[8,1024]{1,0:T(8,128)}) custom-call(bf16[128,1024]{1,0:T(8,128)(2,1)S(1)} %get-tuple-element.6.a, bf16[128,1024]{1,0:T(8,128)(2,1)S(1)} %get-tuple-element.7.b, f32[8,1024]{1,0:T(8,128)S(1)} %get-tuple-element.8.c), custom_call_target="tpu_custom_call" | custom-call | tf_op jit(solution)/shard_map/pallas_call | solution.py:604

commit v5 on v4

--- a/solution.py
+++ b/solution.py
@@ -156,6 +156,9 @@
 
     seven = pl.ds(0, NI - 1)
 
+    def side(h):
+        return lax.rem(my_z + h, 2)
+
     barrier = pltpu.get_barrier_semaphore()
 
     def greet(dev):
@@ -324,6 +327,20 @@
         )
         x_slots[:, mi] = q_rows[mi]
 
+        wait("w2l")
+        wait("w2r")
+        plane_l = whole_w.at[core, my_z, :, :, :, left_w]
+        plane_r = whole_w.at[core, :, my_x, :, :, right_w]
+        some = whole_w.at[core, three, :, :, :, left_w]
+        to_four("w3l", "z", lambda n: plane_l, plane_l, w2_s.at[2], w2_r.at[2], some, some)
+        to_four("w3r", "x", lambda n: plane_r, plane_r, w2_s.at[3], w2_r.at[3], some, some)
+
+
+        wait("cot2")
+        q_cot2[...] = dot(perm_t, r_cot2[...].reshape(SLOTS, 512)).astype(BF).reshape(NG, 16, 512)
+        to_grp("c2", q_cot2, c_slots2, c2_s, c2_r)
+        c_slots2[mg] = q_cot2[mg]
+
         wait("a2")
         wait("a4")
         for q in range(1, 4):
@@ -332,26 +349,6 @@
                 "f%d" % q, ref, ref, f_s.at[q], f_r.at[q],
                 adj_up.at[lax.rem(sib + NI - 2 * q, NI)],
             )
-        wait("cot")
-        q_cot[...] = dot(perm, r_cot[...].reshape(SLOTS, 512)).astype(BF).reshape(NI, 32, 512)
-        to_in(
-            "c", lambda i: q_cot.at[i], c_slots.at[mi], c_s, c_r, q_cot.at[seven], c_slots.at[seven]
-        )
-        c_slots[mi] = q_cot[mi]
-
-        wait("w2l")
-        wait("w2r")
-        plane_l = whole_w.at[core, my_z, :, :, :, left_w]
-        plane_r = whole_w.at[core, :, my_x, :, :, right_w]
-        some = whole_w.at[core, three, :, :, :, left_w]
-        to_four("w3l", "z", lambda n: plane_l, plane_l, w2_s.at[2], w2_r.at[2], some, some)
-        to_four("w3r", "x", lambda n: plane_r, plane_r, w2_s.at[3], w2_r.at[3], some, some)
-
-
-        wait("cot2")
-        q_cot2[...] = dot(perm_t, r_cot2[...].reshape(SLOTS, 512)).astype(BF).reshape(NG, 16, 512)
-        to_grp("c2", q_cot2, c_slots2, c2_s, c2_r)
-        c_slots2[mg] = q_cot2[mg]
 
         wait("v")
         v_sum = v_all[0].astype(F32)
@@ -372,6 +369,13 @@
                 if 0 < j < 4:
                     flipped = adj_up[r, j].astype(F32).T.astype(BF)
                     adj[c * 128:(c + 1) * 128, r * 128:(r + 1) * 128] = flipped
+
+        wait("cot")
+        q_cot[...] = dot(perm, r_cot[...].reshape(SLOTS, 512)).astype(BF).reshape(NI, 32, 512)
+        to_in(
+            "c", lambda i: q_cot.at[i], c_slots.at[mi], c_s, c_r, q_cot.at[seven], c_slots.at[seven]
+        )
+        c_slots[mi] = q_cot[mi]
 
         wait("x")
         feats = jnp.concatenate(
@@ -454,7 +458,7 @@
                 dot(place_t[o], back[o * 128:(o + 1) * 128]).astype(BF).reshape(NI, 32, 128)
             )
         for h in range(2):
-            rows_h = pl.ds(h * 16, 16)
+            rows_h = pl.ds(pl.multiple_of(side(h) * 16, 16), 16)
             to_in(
                 "z1%d" % h, lambda i: z_slots.at[i, :, rows_h], z_mid.at[mi, :, rows_h],
                 z1_s.at[h], z1_r.at[h], z_slots.at[seven, :, rows_h], z_mid.at[seven, :, rows_h],
@@ -495,19 +499,21 @@
         )
         for h in range(2):
             wait("z1%d" % h)
+            n_side = side(h)
+            rows_h = pl.ds(pl.multiple_of(n_side * 16, 16), 16)
             for f in range(NI):
-                z_send[h * 8:(h + 1) * 8, :, f * 128:(f + 1) * 128] = (
-                    dot(perm_z, z_mid[f, :, h * 16:(h + 1) * 16].reshape(ROWS, 128))
+                z_send[pl.ds(n_side * 8, 8), :, f * 128:(f + 1) * 128] = (
+                    dot(perm_z, z_mid[f, :, rows_h].reshape(ROWS, 128))
                     .astype(BF).reshape(8, 16, 128)
                 )
 
             def go(p, carry):
                 n = jnp.bitwise_and(my_gz + p, 7)
-                dest = lax.div(n, 4) * 8 + h * 4 + lax.rem(n, 4)
+                dest = lax.div(n, 4) * 8 + n_side * 4 + lax.rem(n, 4)
 
                 @pl.when(dest != mg)
                 def _():
-                    rcopy(z_send.at[h * 8 + n], z_back.at[mg], z2_s, z2_r, (dest, mi)).start()
+                    rcopy(z_send.at[n_side * 8 + n], z_back.at[mg], z2_s, z2_r, (dest, mi)).start()
 
                 return carry
 

time: 64.9 us -> 60.7 us (0.935)
  the two profiles are of different devices: /device:TPU:3 before, /device:TPU:1 now
where the time goes in v5:
time: 60.7 us; the launch traced here: 60.6 us
  Pallas kernels  59.3 us (98%)
  between operations  1.29 us (2%)
    pallas_call x1, Pallas kernels, per_device(): pl.pallas_call(kernel, out_shape=(pltpu.VMEM((ROWS, D), BF), pltpu.VMEM((...  58.5 us

profile of v5, /device:TPU:1, one launch (start us, length us, event | category | flops | bytes accessed | tf_op | source)
XLA Modules:
  0.0 60.6 jit_solution(780097431527831947)
XLA Ops:
  1.3 58.5 %shard_map.103 = (bf16[128,1024]{1,0:T(8,128)(2,1)S(1)}, bf16[128,1024]{1,0:T(8,128)(2,1)S(1)}, f32[8,1024]{1,0:T(8,128)S(1)}) custom-call(s32[1,10]{1,0:T(1,128)} %cols_hbm.1, s32[1,128]{1,0:T(1,128)} %bitcast.2, s32[1,128]{1,0:T(1,128)} %bitcast.3, s32[1]{0:T(128)S(6)} %copy.11.count_hbm, bf16[128,1024]{1,0:T(8,128)(2,1)} %enc_hbm.1, ...), custom_call_target="tpu_custom_call" | custom-call | tf_op jit(solution)/shard_map/pallas_call | solution.py:595
  59.8 0.8 %shard_map.104 = (bf16[128,1024]{1,0:T(8,128)(2,1)}, bf16[128,1024]{1,0:T(8,128)(2,1)}, f32[8,1024]{1,0:T(8,128)}) custom-call(bf16[128,1024]{1,0:T(8,128)(2,1)S(1)} %get-tuple-element.6.a, bf16[128,1024]{1,0:T(8,128)(2,1)S(1)} %get-tuple-element.7.b, f32[8,1024]{1,0:T(8,128)S(1)} %get-tuple-element.8.c), custom_call_target="tpu_custom_call" | custom-call | tf_op jit(solution)/shard_map/pallas_call | solution.py:610

commit v6 on v5

--- a/solution.py
+++ b/solution.py
@@ -538,6 +538,8 @@
             for n in range(1, 4):
                 half = half + wy_in[2 * n + c]
             wgrad_ref[:, c * 512:(c + 1) * 512] = half * (1.0 / 128)
+        while leaving:
+            leaving.pop(0)()
         wait("z2")
         grad_ref[...] = dot(collect, z_back[...].reshape(SLOTS, D)).astype(BF)
 

time: 60.7 us -> 60.7 us (level)
  no operation moved by 1% of the time
where the time goes in v6:
time: 60.7 us; the launch traced here: 60.6 us
  Pallas kernels  59.3 us (98%)
  between operations  1.29 us (2%)
    pallas_call x1, Pallas kernels, per_device(): pl.pallas_call(kernel, out_shape=(pltpu.VMEM((ROWS, D), BF), pltpu.VMEM((...  58.5 us

profile of v6, /device:TPU:1, one launch (start us, length us, event | category | flops | bytes accessed | tf_op | source)
XLA Modules:
  0.0 60.6 jit_solution(14034805563588121466)
XLA Ops:
  1.3 58.5 %shard_map.103 = (bf16[128,1024]{1,0:T(8,128)(2,1)S(1)}, bf16[128,1024]{1,0:T(8,128)(2,1)S(1)}, f32[8,1024]{1,0:T(8,128)S(1)}) custom-call(s32[1,10]{1,0:T(1,128)} %cols_hbm.1, s32[1,128]{1,0:T(1,128)} %bitcast.2, s32[1,128]{1,0:T(1,128)} %bitcast.3, s32[1]{0:T(128)S(6)} %copy.11.count_hbm, bf16[128,1024]{1,0:T(8,128)(2,1)} %enc_hbm.1, ...), custom_call_target="tpu_custom_call" | custom-call | tf_op jit(solution)/shard_map/pallas_call | solution.py:597
  59.7 0.8 %shard_map.104 = (bf16[128,1024]{1,0:T(8,128)(2,1)}, bf16[128,1024]{1,0:T(8,128)(2,1)}, f32[8,1024]{1,0:T(8,128)}) custom-call(bf16[128,1024]{1,0:T(8,128)(2,1)S(1)} %get-tuple-element.6.a, bf16[128,1024]{1,0:T(8,128)(2,1)S(1)} %get-tuple-element.7.b, f32[8,1024]{1,0:T(8,128)S(1)} %get-tuple-element.8.c), custom_call_target="tpu_custom_call" | custom-call | tf_op jit(solution)/shard_map/pallas_call | solution.py:612
